TPU v7x, 128 devices: a whole 4x4x4 slice. The times are simulated.
128 devices in a mesh: lon: 32 (over x, z, core), bin: 4 (over y).
Axes of the slice: x: 4, y: 4, z: 4, core: 2. Of those that a mesh axis runs over, the one named last changes fastest.
Arguments:
- spectrum: float32 [1296, 1440, 128], P('bin', 'lon'), may hold values from 0.05 to 1
- sea_mask: int32 [1440, 128], P('lon'), may hold values from 0 to 1, as said below
- cour_lon: float32 [1296, 128], P('bin'), may hold values from -0.45 to 0.45
- cour_lat: float32 [1296], P('bin'), may hold values from -0.45 to 0.45
- wind: float32 [1440, 128], P('lon'), may hold values from 0.5 to 2
- growth_rate: float32 [1296], replicated, may hold values from 0.05 to 0.5
- band_weight: float32 [1296], replicated, may hold values from 0.00038580247 to 0.0030864198
- freq_mix: float32 [36, 36], replicated, may hold values from -1 to 1
- dir_mix: float32 [36, 36], replicated, may hold values from -1 to 1
- routes: int32 [32, 128, 32], P('lon'), may hold values from 0 to 5759, as said below
- counts: int32 [32, 128], P('lon'), may hold values from 0 to 32, as said below
Outputs:
- new_spectrum: float32 [1296, 1440, 128], P('bin', 'lon')
Inputs may be any that keep to these rules, and one draw needn't show every extreme that they name: `routes`: for block g and owner o, entries s < counts[g, o] name distinct cells of block g; together they name every sea cell of the block once; unused entries are 0. `counts`: in every draw one owner gets 32 cells from every block. `sea_mask`: 1 exactly at the cells named by routes; a block holds from 2048 to 4096 sea cells, some block exactly the latter.
All inputs are finite; a program needn't handle non-finite values.
Results may differ from a plain program's by a relative error of at most 0.0001.
Values sent between devices are 32-bit elements; how exact they have to be, the bound alone decides.
A program may use at most 128 MiB of HBM per device.

v0:
```python
import jax
import jax.numpy as jnp
from jax import lax
from jax.sharding import PartitionSpec as P

dissipation = 0.5
time_step = 0.5


def with_halo(block, sides, width):
    for axis, dim in sides:
        count = lax.axis_size(axis)
        forward = [(i, i + 1) for i in range(count - 1)]
        forward.append((count - 1, 0))
        backward = [(target, source) for source, target in forward]
        low = lax.ppermute(
            lax.slice_in_dim(block, block.shape[dim] - width, None, axis=dim), axis, forward
        )
        high = lax.ppermute(lax.slice_in_dim(block, 0, width, axis=dim), axis, backward)
        block = jnp.concatenate([low, block, high], axis=dim)
    return block


def advect(padded, cour_lon, cour_lat):
    middle = padded[:, 1:-1, :]
    west = padded[:, :-2, :]
    east = padded[:, 2:, :]
    zero = jnp.zeros_like(middle[:, :, :1])
    south = jnp.concatenate([zero, middle[:, :, :-1]], axis=2)
    north = jnp.concatenate([middle[:, :, 1:], zero], axis=2)
    along = cour_lon[:, None, :]
    across = cour_lat[:, None, None]
    return (
        middle
        - jnp.maximum(along, 0.0) * (middle - west)
        - jnp.minimum(along, 0.0) * (east - middle)
        - jnp.maximum(across, 0.0) * (middle - south)
        - jnp.minimum(across, 0.0) * (north - middle)
    )


def sources(full, speed, growth_rate, band_weight, freq_mix, dir_mix):
    steep = jnp.sum(band_weight[:, None] * full, axis=0)
    factor = growth_rate[:, None] * speed[None, :] - dissipation * steep / (1.0 + steep)
    cube = full.reshape(freq_mix.shape[0], dir_mix.shape[0], full.shape[1])
    mixed = jnp.einsum("fg,gdm->fdm", freq_mix, cube, precision=lax.Precision.HIGHEST)
    mixed = jnp.einsum("de,fem->fdm", dir_mix, mixed, precision=lax.Precision.HIGHEST)
    return full * factor + mixed.reshape(full.shape)


def on_device(
    spectrum,
    sea_mask,
    cour_lon,
    cour_lat,
    wind,
    growth_rate,
    band_weight,
    freq_mix,
    dir_mix,
    routes,
    counts,
):
    bins, width, rows = spectrum.shape
    cells = width * rows
    sea = sea_mask.astype(jnp.float32)
    masked = spectrum * sea[None]
    padded = with_halo(masked, (("lon", 1),), 1)
    moved = advect(padded, cour_lon, cour_lat) * sea[None]
    flat = moved.reshape(bins, cells)
    wind_flat = wind.reshape(cells)
    owners = routes.shape[1]
    capacity = routes.shape[2]
    slots = routes[0].reshape(owners * capacity)
    valid = (jnp.arange(capacity)[None, :] < counts[0][:, None]).reshape(owners * capacity)
    groups = lax.axis_size("bin")
    sending = flat[:, slots].reshape(bins, owners, capacity)
    gust_send = wind_flat[slots].reshape(1, owners, capacity)
    arrived = lax.all_to_all(sending, ("lon", "bin"), split_axis=1, concat_axis=1, tiled=True)
    gusts = lax.all_to_all(gust_send, ("lon", "bin"), split_axis=1, concat_axis=1, tiled=True)
    count_here = arrived.shape[2]
    blocks = owners // groups
    whole = arrived.reshape(bins, blocks, groups, count_here).transpose(2, 0, 1, 3)
    whole = whole.reshape(bins * groups, blocks * count_here)
    speed = gusts.reshape(blocks, groups, count_here)[:, 0, :].reshape(blocks * count_here)
    source = sources(whole, speed, growth_rate, band_weight, freq_mix, dir_mix)
    outgoing = source.reshape(groups, bins, blocks, count_here).transpose(1, 2, 0, 3)
    outgoing = outgoing.reshape(bins, owners, count_here)
    returned = lax.all_to_all(outgoing, ("lon", "bin"), split_axis=1, concat_axis=1, tiled=True)
    kept_terms = jnp.where(valid[None, :], returned.reshape(bins, owners * capacity), 0.0)
    term = jnp.zeros((bins, cells), jnp.float32).at[:, slots].add(kept_terms)
    updated = flat + time_step * term
    return updated.reshape(bins, width, rows)


def solution(mesh):
    placed = (
        P("bin", "lon", None),
        P("lon", None),
        P("bin", None),
        P("bin"),
        P("lon", None),
        P(),
        P(),
        P(),
        P(),
        P("lon", None, None),
        P("lon", None),
    )
    return jax.shard_map(
        on_device, mesh=mesh, in_specs=placed, out_specs=P("bin", "lon", None), check_vma=False
    )
```

profile of v0, /device:TPU:1, one launch (start us, length us, event | category | flops | bytes accessed | tf_op | source)
XLA Modules:
  0.0 433.1 jit_solution(14650588762731884162)
XLA Ops:
  0.0 0.0 copy-start
  0.0 0.7 convert_element_type.3
  0.8 0.0 copy-start.7
  0.8 3.8 broadcast_multiply_fusion
  4.5 0.0 copy-start.2
  4.5 3.1 copy-done.2
  7.7 3.1 collective-permute-start
  10.8 0.0 collective-permute-start.1
  10.8 0.0 copy-done.7
  10.8 0.1 copy.20
  10.9 0.1 reshape_squeeze.3
  11.0 0.0 copy-done
  11.0 23.0 %gather_fusion.1 = f32[4096]{0:T(1024)S(1)} fusion(f32[5760]{0:T(1024)S(1)} %bitcast.36, s32[4096]{0:T(1024)S(1)} %broadcast_clamp_fusion), kind=kCustom, calls=%fused_computation.1 | custom fusion | bytes 49152 | tf_op jit(solution)/shard_map/gather | solution.py:78
  34.1 0.7 reshape.122
  34.8 10.2 %all-to-all-start.1 = ((f32[1,128,32]{2,0,1:T(1,128)}), f32[1,128,32]{2,0,1:T(1,128)S(1)}, u32[]{:S(2)}, u32[]{:S(2)}) async-start(f32[1,128,32]{2,0,1:T(1,128)} %bitcast.8), calls=%async_computation.1 | async-start | bytes 131072 | tf_op jit(solution)/shard_map/all_to_all | solution.py:80
  45.0 0.0 copy-start.4
  45.0 0.0 copy-start.10
  45.0 12.7 %fusion.24 = (f32[324,45,127]{2,0,1:T(8,128)}, f32[324,45,127]{2,0,1:T(8,128)}) fusion(f32[324,45,128]{2,0,1:T(8,128)} %copy-done.2), kind=kLoop, calls=%fused_computation.38 | loop fusion | bytes 29626560 | tf_op jit(solution)/shard_map/slice | solution.py:29
  57.7 0.0 copy-done.4
  57.7 0.0 copy-done.10
  57.7 0.0 collective-permute-done
  57.8 0.0 collective-permute-done.1
  57.8 17.2 %fusion.5 = f32[324,45,128]{2,0,1:T(8,128)} fusion(f32[324,45,128]{2,0,1:T(8,128)} %copy-done.2, f32[324,1,128]{2,0,1:T(8,128)S(1)} %collective-permute-done.1, f32[324,1,128]{2,0,1:T(8,128)S(1)} %collective-permute-done, f32[324,45,127]{2,0,1:T(8,128)} %get-tuple-element.6, f32[324,45,127]{2,0,1:T(8,128)} %get-tuple-element.5, ...), kind=kLoop, calls=%fused_computation.10 | loop fusion | flops 27993600 | bytes 30432384 | tf_op jit(solution)/shard_map/mul | solution.py:69
  74.9 9.0 %copy.19 = f32[324,45,128]{0,2,1:T(8,128)} copy(f32[324,45,128]{2,0,1:T(8,128)} %fusion.5) | data formatting | bytes 14929920 | tf_op jit(solution)/shard_map/mul | solution.py:69
  84.0 20.6 %gather_fusion = f32[4096,324]{1,0:T(8,128)} fusion(f32[324,5760]{0,1:T(8,128)} %bitcast.37, s32[4096]{0:T(1024)S(1)} %broadcast_clamp_fusion), kind=kCustom, calls=%fused_computation | custom fusion | bytes 10633216 | tf_op jit(solution)/shard_map/gather | solution.py:77
  104.5 0.0 copy-start.8
  104.5 0.0 copy-start.9
  104.5 0.0 all-to-all-done.1
  104.5 10.2 %all-to-all-start = ((f32[324,128,32]{0,2,1:T(8,128)}), f32[324,128,32]{0,2,1:T(8,128)}, u32[]{:S(2)}, u32[]{:S(2)}) async-start(f32[324,128,32]{0,2,1:T(8,128)} %bitcast.40), calls=%async_computation | async-start | bytes 12582912 | tf_op jit(solution)/shard_map/all_to_all | solution.py:79
  114.7 0.0 copy-done.8
  114.7 0.1 mul.111
  114.8 0.0 copy-done.9
  114.8 0.1 mul.106
  114.9 79.2 %all-to-all-done = f32[324,128,32]{0,2,1:T(8,128)} async-done(((f32[324,128,32]{0,2,1:T(8,128)}), f32[324,128,32]{0,2,1:T(8,128)}, u32[]{:S(2)}, u32[]{:S(2)}) %all-to-all-start) | async-done | bytes 5308448 | tf_op jit(solution)/shard_map/all_to_all | solution.py:79
  194.1 20.2 %copy.22 = f32[4,324,32,32]{3,2,1,0:T(8,128)} copy(f32[4,324,32,32]{1,3,0,2:T(8,128)} %bitcast.6) | data formatting | bytes 10616832 | tf_op jit(solution)/shard_map/transpose | solution.py:83
  214.3 0.0 copy-start.5
  214.3 17.1 %reshape_reshape.3 = f32[36,36,1024]{2,1,0:T(8,128)} reshape(f32[4,324,32,32]{3,2,1,0:T(8,128)} %copy.22) | data formatting | bytes 10616832 | tf_op jit(solution)/shard_map/reshape;reshape | solution.py:45
  231.4 0.0 copy-done.5
  231.4 0.0 copy-start.6
  231.4 13.1 %fusion.16 = f32[36,36,1024]{2,0,1:T(8,128)S(1)} fusion(f32[36,36,1024]{2,1,0:T(8,128)} %reshape_reshape.3, f32[36,36]{1,0:T(8,128)S(1)} %copy-done.5), kind=kOutput, calls=%fused_computation.26 | convolution fusion | flops 573308928 | bytes 10622016 | tf_op jit(solution)/shard_map/fg,gdm->fdm/dot_general | solution.py:46
  244.5 0.0 copy-done.6
  244.5 10.6 %fusion.19 = f32[36,36,1024]{2,1,0:T(8,128)} fusion(f32[36,36,1024]{2,0,1:T(8,128)S(1)} %fusion.16, f32[36,36]{1,0:T(8,128)S(1)} %copy-done.6), kind=kOutput, calls=%fused_computation.27 | convolution fusion | flops 573308928 | bytes 10622016 | tf_op jit(solution)/shard_map/de,fem->fdm/dot_general | solution.py:47
  255.0 14.5 %reshape.124 = f32[4,324,32,32]{3,2,1,0:T(8,128)} reshape(f32[36,36,1024]{2,1,0:T(8,128)} %fusion.19) | data formatting | bytes 10616832 | tf_op jit(solution)/shard_map/reshape | solution.py:48
  269.6 15.7 %copy.25 = f32[4,324,32,32]{1,3,0,2:T(8,128)} copy(f32[4,324,32,32]{3,2,1,0:T(8,128)} %reshape.124) | data formatting | bytes 10616832 | tf_op jit(solution)/shard_map/reshape | solution.py:48
  285.2 0.0 copy-start.3
  285.2 3.5 multiply_reduce_fusion
  288.8 1.1 copy-done.3
  289.8 5.3 %multiply_add_fusion.1 = f32[4,324,32,32]{1,3,0,2:T(8,128)} fusion(f32[4,324,32,32]{1,3,0,2:T(8,128)S(1)} %copy-done.3, f32[32,32]{1,0:T(8,128)S(1)} %add_divide_fusion, f32[32,32]{1,0:T(8,128)S(1)} %bitcast.44, f32[4,324]{1,0:T(4,128)S(1)} %mul.106, f32[324,128,32]{0,2,1:T(8,128)} %all-to-all-done), kind=kLoop, calls=%fused_computation.18 | loop fusion | flops 5308416 | bytes 15938624 | tf_op jit(solution)/shard_map/add | solution.py:48
  295.1 0.0 copy-start.11
  295.1 4.9 %all-to-all-start.2 = ((f32[324,128,32]{0,2,1:T(8,128)}), f32[324,128,32]{0,2,1:T(8,128)}, u32[]{:S(2)}, u32[]{:S(2)}) async-start(f32[324,128,32]{0,2,1:T(8,128)} %bitcast.39), calls=%async_computation.2 | async-start | bytes 12582912 | tf_op jit(solution)/shard_map/all_to_all | solution.py:89
  300.0 0.0 copy-done.11
  300.0 0.1 iota_compare_fusion
  300.1 0.1 lt.39
  300.2 79.2 %all-to-all-done.2 = f32[324,128,32]{0,2,1:T(8,128)} async-done(((f32[324,128,32]{0,2,1:T(8,128)}), f32[324,128,32]{0,2,1:T(8,128)}, u32[]{:S(2)}, u32[]{:S(2)}) %all-to-all-start.2) | async-done | bytes 5308448 | tf_op jit(solution)/shard_map/all_to_all | solution.py:89
  379.4 4.9 %bitcast_select_fusion = f32[324,4096]{0,1:T(8,128)} fusion(f32[324,128,32]{0,2,1:T(8,128)} %all-to-all-done.2, pred[4096]{0:T(1024)(128)(4,1)S(1)} %lt.39), kind=kLoop, calls=%fused_computation.17 | loop fusion | flops 1327104 | bytes 10620928 | tf_op jit(solution)/shard_map/jit(_where)/select_n | solution.py:90
  384.3 29.4 %scatter_custom_fusion = f32[324,5760]{0,1:T(8,128)} fusion(s32[4096]{0:T(1024)S(1)} %bitcast.43, f32[324,4096]{0,1:T(8,128)} %bitcast_select_fusion, f32[]{:T(128)} %constant.5.clone.1), kind=kCustom, calls=%fused_computation.15 | custom fusion | flops 1327104 | bytes 12773380 | tf_op jit(solution)/shard_map/scatter-add | solution.py:91
  413.8 10.3 %multiply_add_fusion = f32[324,5760]{0,1:T(8,128)} fusion(f32[324,5760]{0,1:T(8,128)} %scatter_custom_fusion, f32[324,45,128]{0,2,1:T(8,128)} %copy.19), kind=kLoop, calls=%fused_computation.3 | loop fusion | flops 3732480 | bytes 22394880 | tf_op jit(solution)/shard_map/add | solution.py:92
  424.1 0.0 copy-start.1
  424.1 9.0 %copy.26 = f32[324,45,128]{2,0,1:T(8,128)} copy(f32[324,45,128]{0,2,1:T(8,128)} %bitcast.38) | data formatting | bytes 14929920 | tf_op jit(solution)/shard_map/reshape | solution.py:93
  433.1 0.0 copy-done.1
  (7 shorter events, 0.1 us)
Async XLA Ops:
  0.0 11.0 %copy-start = (f32[45,128]{1,0:T(8,128)S(1)}, f32[45,128]{1,0:T(8,128)}, u32[]{:S(2)}) copy-start(f32[45,128]{1,0:T(8,128)} %param.15) | copy-start | bytes 69124
  0.8 10.0 %copy-start.7 = (s32[1,128,32]{1,2,0:T(8,128)S(1)}, s32[1,128,32]{1,2,0:T(8,128)}, u32[]{:S(2)}) copy-start(s32[1,128,32]{1,2,0:T(8,128)} %param.20) | copy-start | bytes 49156
  4.5 3.1 copy-start.2
  7.7 50.1 %collective-permute-start = (f32[324,1,128]{2,0,1:T(8,128)S(1)}, f32[324,1,128]{2,0,1:T(8,128)S(1)}, u32[]{:S(2)}, u32[]{:S(2)}) collective-permute-start(f32[324,1,128]{2,0,1:T(8,128)S(1)} %get-tuple-element.7), channel_id=1, source_target_pairs={{0,4},{4,8},{8,12},{12,16},{16,20},{20,24},{24,28},{28,32},{32,36}... | collective-permute-start | bytes 497672 | tf_op jit(solution)/shard_map/ppermute | solution.py:16
  10.8 47.0 %collective-permute-start.1 = (f32[324,1,128]{2,0,1:T(8,128)S(1)}, f32[324,1,128]{2,0,1:T(8,128)S(1)}, u32[]{:S(2)}, u32[]{:S(2)}) collective-permute-start(f32[324,1,128]{2,0,1:T(8,128)S(1)} %get-tuple-element.8), channel_id=1, source_target_pairs={{4,0},{8,4},{12,8},{16,12},{20,16},{24,20},{28,24},{32,28},{36,32}... | collective-permute-start | bytes 497672 | tf_op jit(solution)/shard_map/ppermute | solution.py:19
  34.8 69.8 %all-to-all-start.1 = ((f32[1,128,32]{2,0,1:T(1,128)}), f32[1,128,32]{2,0,1:T(1,128)S(1)}, u32[]{:S(2)}, u32[]{:S(2)}) async-start(f32[1,128,32]{2,0,1:T(1,128)} %bitcast.8), calls=%async_computation.1 | async-start | bytes 131072 | tf_op jit(solution)/shard_map/all_to_all | solution.py:80
  45.0 12.7 %copy-start.4 = (f32[324,128]{1,0:T(8,128)S(1)}, f32[324,128]{1,0:T(8,128)}, u32[]{:S(2)}) copy-start(f32[324,128]{1,0:T(8,128)} %param.13) | copy-start | bytes 497668
  45.0 12.7 %copy-start.10 = (f32[324]{0:T(512)S(1)}, f32[324]{0:T(512)}, u32[]{:S(2)}) copy-start(f32[324]{0:T(512)} %param.14) | copy-start | bytes 3892
  104.5 10.2 %copy-start.8 = (f32[1296]{0:T(1024)S(1)}, f32[1296]{0:T(1024)}, u32[]{:S(2)}) copy-start(f32[1296]{0:T(1024)} %param.17) | copy-start | bytes 15556
  104.5 10.3 %copy-start.9 = (f32[1296]{0:T(1024)S(1)}, f32[1296]{0:T(1024)}, u32[]{:S(2)}) copy-start(f32[1296]{0:T(1024)} %param.16) | copy-start | bytes 15556
  104.5 89.6 %all-to-all-start = ((f32[324,128,32]{0,2,1:T(8,128)}), f32[324,128,32]{0,2,1:T(8,128)}, u32[]{:S(2)}, u32[]{:S(2)}) async-start(f32[324,128,32]{0,2,1:T(8,128)} %bitcast.40), calls=%async_computation | async-start | bytes 12582912 | tf_op jit(solution)/shard_map/all_to_all | solution.py:79
  214.3 17.1 %copy-start.5 = (f32[36,36]{1,0:T(8,128)S(1)}, f32[36,36]{1,0:T(8,128)}, u32[]{:S(2)}) copy-start(f32[36,36]{1,0:T(8,128)} %param.18) | copy-start | bytes 15556
  231.4 13.1 %copy-start.6 = (f32[36,36]{1,0:T(8,128)S(1)}, f32[36,36]{1,0:T(8,128)}, u32[]{:S(2)}) copy-start(f32[36,36]{1,0:T(8,128)} %param.19) | copy-start | bytes 15556
  285.2 4.6 %copy-start.3 = (f32[4,324,32,32]{1,3,0,2:T(8,128)S(1)}, f32[4,324,32,32]{1,3,0,2:T(8,128)}, u32[]{:S(2)}) copy-start(f32[4,324,32,32]{1,3,0,2:T(8,128)} %copy.25) | copy-start | bytes 15925252
  295.1 4.9 %copy-start.11 = (s32[1,128]{1,0:T(1,128)S(1)}, s32[1,128]{1,0:T(1,128)}, u32[]{:S(2)}) copy-start(s32[1,128]{1,0:T(1,128)} %param.21) | copy-start | bytes 1540
  295.1 84.3 %all-to-all-start.2 = ((f32[324,128,32]{0,2,1:T(8,128)}), f32[324,128,32]{0,2,1:T(8,128)}, u32[]{:S(2)}, u32[]{:S(2)}) async-start(f32[324,128,32]{0,2,1:T(8,128)} %bitcast.39), calls=%async_computation.2 | async-start | bytes 12582912 | tf_op jit(solution)/shard_map/all_to_all | solution.py:89
  424.1 9.0 %copy-start.1 = (f32[45,128]{1,0:T(8,128)S(1)}, f32[45,128]{1,0:T(8,128)}, u32[]{:S(2)}) copy-start(f32[45,128]{1,0:T(8,128)} %param.15) | copy-start | bytes 69124
where the time goes:
time: 435 us; the launch traced here: 433 us
  waiting for transfers between devices  158 us (36%)
  local copies, waits for them, and re-layouts  147 us (34%)
  other arithmetic  75.3 us (17%)
  starting transfers between devices  28.4 us (7%)
  matrix products  23.7 us (5%)
    all_to_all x1, waiting for transfers between devices, on_device(): lax.all_to_all(sending, ('lon', 'bin'), split_axis=1, concat_axis=1, tile...  79.2 us
    all_to_all x1, waiting for transfers between devices, on_device(): lax.all_to_all(outgoing, ('lon', 'bin'), split_axis=1, concat_axis=1, til...  79.2 us
    reshape x2, local copies, waits for them, and re-layouts, sources(): return full * factor + mixed.reshape(full.shape)  30.2 us
    scatter-add x1, other arithmetic, on_device(): term = jnp.zeros((bins, cells), jnp.float32).at[:, slots].add(kept_terms)  29.4 us
    gather x1, local copies, waits for them, and re-layouts, on_device(): gust_send = wind_flat[slots].reshape(1, owners, capacity)  23 us
    gather x1, local copies, waits for them, and re-layouts, on_device(): sending = flat[:, slots].reshape(bins, owners, capacity)  20.6 us
    transpose x1, local copies, waits for them, and re-layouts, on_device(): arrived.reshape(bins, blocks, groups, count_here).transpose(2, 0, 1, 3)  20.2 us
    mul x1, other arithmetic, on_device(): moved = advect(padded, cour_lon, cour_lat) * sea[None]  17.2 us
  transfers between devices with their start and end apart: 5, of which 2 were waited for; matrix products, arithmetic and copies ran while one was open for 19% of the time, Pallas kernels for 0%

commit v1 on v0

v1 whole, which is shorter than its diff:
```python
import functools

import jax
import jax.numpy as jnp
import numpy as np
from jax import lax
from jax.experimental import pallas as pl
from jax.experimental.pallas import tpu as pltpu
from jax.sharding import PartitionSpec as P

MESH = pl.DeviceIdType.MESH
NF, ND = 36, 36
LON, LAT = 45, 128
GROUPS = 4
LOCAL = 324
PADDED = 328
CELLS = 4096
SHARE = CELLS // GROUPS
TILES = CELLS // LAT
SIZES = (64, 64, 64, 64, 72)
STARTS = (0, 64, 128, 192, 256)
PARTS = len(SIZES)
KSTARTS = tuple(GROUPS * s for s in STARTS)
KTOTAL = GROUPS * PADDED
MROWS = 336
UNROLL = 6


def column_maps():
    freq = np.zeros((NF, KTOTAL), np.float32)
    direction = np.zeros((ND, KTOTAL), np.float32)
    at = 0
    for start, size in zip(STARTS, SIZES):
        for p in range(GROUPS):
            for b in range(start, start + size):
                if b < LOCAL:
                    k = p * LOCAL + b
                    freq[k // ND, at] = 1.0
                    direction[k % ND, at] = 1.0
                at += 1
    return freq, direction


def tables(sea_mask):
    sea = jnp.roll(sea_mask.astype(jnp.float32), -1, axis=0)
    lanes = jnp.arange(LAT)
    upto = (lanes[:, None] <= lanes[None, :]).astype(jnp.float32)
    rank = jnp.dot(sea, upto).astype(jnp.int32)
    number = rank[:, -1].astype(jnp.float32)
    steps = jnp.arange(LON + 1)
    before = (steps[:, None] > steps[None, :LON]).astype(jnp.float32)
    offset_all = jnp.sum(before * number[None, :], axis=1).astype(jnp.int32)
    offset = offset_all[:LON]
    shift = offset % LAT
    wanted = (lanes[None, :] - shift[:, None]) % LAT
    source = jnp.sum((rank[:, :, None] <= wanted[:, None, :]).astype(jnp.int32), axis=1)
    source = jnp.minimum(source, LAT - 1)
    low = (lanes[None, :] >= shift[:, None]).astype(jnp.int32)
    cross = jnp.broadcast_to((shift[:, None] + rank[:, -1:] >= LAT).astype(jnp.int32), (LON, LAT))
    ends = jnp.arange(TILES) * LAT + LAT - 1
    last = jnp.sum((offset_all[None, :] <= ends[:, None]).astype(jnp.int32), axis=1) - 1
    first = jnp.minimum(offset // LAT, TILES - 1)
    place = (shift[:, None] + rank - 1) % LAT

    def wide(a):
        return jnp.broadcast_to(a[:, None, :], (a.shape[0], 8, LAT))

    return wide(sea), wide(source), wide(low), wide(cross), last, first, wide(place)


def exchange_kernel(
    last_ref, spec_ref, coef_ref, sea_ref, source_ref, low_ref, cross_ref, fmix_ref, dmix_ref, fcol_ref, dcol_ref,
    moved_ref, mixed_ref, damp_ref,
    x, halo, sea_halo, packed, stage, recv_a, recv_b, acc, w_hi_a, w_lo_a, w_hi_b, w_lo_b, fcols, dcols,
    steep, sums,
    in_sem, out_sem, halo_send, halo_recv, send_sem, recv_sem, back_send, back_recv, sum_send, sum_recv, own_sem,
):
    me = lax.axis_index("bin")
    block = lax.axis_index("lon")
    blocks = lax.axis_size("lon")
    west = lax.rem(block + blocks - 1, blocks)
    east = lax.rem(block + 1, blocks)

    def peer(d):
        return lax.rem(me + d, GROUPS)

    loads = []
    for c in range(PARTS):
        rows = min(SIZES[c], LOCAL - STARTS[c])
        copy = pltpu.make_async_copy(
            spec_ref.at[:, pl.ds(STARTS[c], rows), :], x.at[:, pl.ds(STARTS[c], rows), :], in_sem.at[c]
        )
        copy.start()
        loads.append(copy)

    barrier = pltpu.get_barrier_semaphore()
    for d in (1, 2, 3):
        pl.semaphore_signal(barrier, inc=1, device_id=(block, peer(d)), device_id_type=MESH)
    pl.semaphore_signal(barrier, inc=1, device_id=(west, me), device_id_type=MESH)
    pl.semaphore_signal(barrier, inc=1, device_id=(east, me), device_id_type=MESH)
    pl.semaphore_wait(barrier, 5)

    edges = []
    for slot, row, step, to in ((0, LON - 1, LON - 2, east), (1, 0, LON - 1, west)):
        copy = pltpu.make_async_remote_copy(
            src_ref=spec_ref.at[row], dst_ref=halo.at[slot, pl.ds(0, LOCAL), :],
            send_sem=halo_send.at[slot], recv_sem=halo_recv.at[slot], device_id=(to, me), device_id_type=MESH,
        )
        copy.start()
        edges.append(copy)
        copy = pltpu.make_async_remote_copy(
            src_ref=sea_ref.at[step], dst_ref=sea_halo.at[slot],
            send_sem=halo_send.at[2 + slot], recv_sem=halo_recv.at[2 + slot], device_id=(to, me), device_id_type=MESH,
        )
        copy.start()
        edges.append(copy)

    steep[...] = jnp.zeros_like(steep)
    pad = PADDED - LOCAL
    x[:, pl.ds(LOCAL, pad), :] = jnp.zeros((LON, pad, LAT), jnp.float32)
    halo[:, pl.ds(LOCAL, pad), :] = jnp.zeros((2, pad, LAT), jnp.float32)

    def advect_rows(start, n, base):
        at = [pl.ds(pl.multiple_of(base + 8 * j, 8), 8) for j in range(n)]
        to = [pl.ds(pl.multiple_of(base - start + 8 * j, 8), 8) for j in range(n)]
        coef = [[coef_ref[q, at[j], :] for q in range(6)] for j in range(n)]

        def finish(i, row, low_side, mid, high_side, hold):
            sea = sea_ref[i]
            source = source_ref[i]
            low = low_ref[i] != 0
            cross = cross_ref[i] != 0
            total = steep[i]
            new_hold = []
            for j in range(n):
                c0, cw, ce, cs, cn, weight = coef[j]
                m = mid[j]
                value = c0 * m + cw * low_side[j] + ce * high_side[j]
                value = value + cs * pltpu.roll(m, 1, 1) + cn * pltpu.roll(m, LAT - 1, 1)
                value = value * sea
                x[row, at[j], :] = value
                total = total + weight * value
                turned = jnp.take_along_axis(value, source, axis=1)
                kept = jnp.where(low, turned, hold[j])
                packed[i, to[j], :] = kept
                new_hold.append(jnp.where(cross, turned, kept))
            steep[i] = total
            return tuple(new_hold)

        first = tuple(x[0, at[j], :] * sea_ref[LON - 1] for j in range(n))
        second = tuple(x[1, at[j], :] * sea_ref[0] for j in range(n))
        zero = tuple(jnp.zeros((8, LAT), jnp.float32) for j in range(n))

        def one(i, carry):
            low_side, mid, hold = carry
            sea_next = sea_ref[i + 1]
            high_side = tuple(x[i + 2, at[j], :] * sea_next for j in range(n))
            hold = finish(i, i + 1, low_side, mid, high_side, hold)
            return (mid, high_side, hold)

        def several(s, carry):
            for u in range(UNROLL):
                carry = one(s * UNROLL + u, carry)
            return carry

        carry = (first, second, zero)
        carry = lax.fori_loop(0, (LON - 3) // UNROLL, several, carry)
        carry = one(LON - 3, carry)
        low_side, mid, hold = carry
        high_side = tuple(halo[1, at[j], :] * sea_halo[1] for j in range(n))
        hold = finish(LON - 2, LON - 1, low_side, mid, high_side, hold)
        low_side = tuple(halo[0, at[j], :] * sea_halo[0] for j in range(n))
        hold = finish(LON - 1, 0, low_side, first, second, hold)
        for j in range(n):
            packed[LON, to[j], :] = hold[j]

    sends = []
    stores = []
    for c in range(PARTS):
        start, size = STARTS[c], SIZES[c]
        n = 2 if size % 16 == 0 else 3
        loads[c].wait()
        if c == 0:
            for copy in edges:
                copy.wait()

        def group(s, _, start=start, n=n):
            advect_rows(start, n, start + s * 8 * n)
            return 0

        lax.fori_loop(0, size // (8 * n), group, 0)
        rows = min(size, LOCAL - start)
        copy = pltpu.make_async_copy(
            x.at[:, pl.ds(start, rows), :], moved_ref.at[:, pl.ds(start, rows), :], out_sem.at[c]
        )
        copy.start()
        stores.append(copy)
        recv = recv_b if c == PARTS - 1 else recv_a.at[c]
        mine = pl.ds(pl.multiple_of(me * size, 8), size)
        for d in (2, 1, 3, 0):
            to = peer(d)
            for k in range(SHARE // LAT):
                row = last_ref[to * (SHARE // LAT) + k]
                value = packed[row, pl.ds(0, size), :]
                lanes = pl.ds(k * LAT, LAT)
                if d == 0:
                    recv[mine, lanes] = value
                else:
                    stage[d - 1, pl.ds(start, size), lanes] = value
            if d:
                copy = pltpu.make_async_remote_copy(
                    src_ref=stage.at[d - 1, pl.ds(start, size), :], dst_ref=recv.at[mine, :],
                    send_sem=send_sem.at[c, d - 1], recv_sem=recv_sem.at[c, d - 1],
                    device_id=(block, to), device_id_type=MESH,
                )
                copy.start()
                sends.append((c, copy))

    sums[0] = jnp.sum(steep[...], axis=1)
    sum_copies = []
    for d in (1, 2, 3):
        copy = pltpu.make_async_remote_copy(
            src_ref=sums.at[0], dst_ref=sums.at[d], send_sem=sum_send.at[d - 1], recv_sem=sum_recv.at[d - 1],
            device_id=(block, peer(d)), device_id_type=MESH,
        )
        copy.start()
        sum_copies.append(copy)

    exact = functools.partial(jnp.dot, precision=lax.Precision.HIGHEST, preferred_element_type=jnp.float32)
    fcols[...] = exact(fmix_ref[...], fcol_ref[...])
    spread = exact(dmix_ref[...], dcol_ref[...])
    for j in range(4):
        dcols[pl.ds(j * ND, ND), :] = spread

    def matrix_rows(p, _):
        for g, (size, count) in enumerate(((144, 4), (144, 4), (48, 1))):
            for c in range(PARTS):
                width = GROUPS * SIZES[c]
                cols = pl.ds(KSTARTS[c], width)
                index = lax.broadcasted_iota(jnp.int32, (size, width), 0)
                rows = [fcols[pl.ds(p * 9 + 4 * g + j, 1), cols] for j in range(count)]
                if count == 1:
                    factor = jnp.where(index < ND, rows[0], 0.0)
                else:
                    factor = jnp.where(
                        index < 2 * ND,
                        jnp.where(index < ND, rows[0], rows[1]),
                        jnp.where(index < 3 * ND, rows[2], rows[3]),
                    )
                value = factor * dcols[pl.ds(0, size), cols]
                high = value.astype(jnp.bfloat16)
                low = (value - high.astype(jnp.float32)).astype(jnp.bfloat16)
                at = pl.ds(144 * g, size)
                if c == PARTS - 1:
                    w_hi_b[p, at, :] = high
                    w_lo_b[p, at, :] = low
                else:
                    w_hi_a[c, p, at, :] = high
                    w_lo_a[c, p, at, :] = low
        return 0

    lax.fori_loop(0, GROUPS, matrix_rows, 0)

    dot = functools.partial(jnp.dot, preferred_element_type=jnp.float32)

    def halves(value):
        high = value.astype(jnp.bfloat16)
        return high, (value - high.astype(jnp.float32)).astype(jnp.bfloat16)

    for c in range(PARTS - 1):
        for at, copy in sends:
            if at == c:
                copy.wait_recv()

        def columns(s, _, c=c):
            lanes = pl.ds(pl.multiple_of(s * 256, 256), 256)
            high, low = halves(recv_a[c, :, lanes])

            def rows(p, _):
                value = dot(w_hi_a[c, p], high) + dot(w_lo_a[c, p], high) + dot(w_hi_a[c, p], low)
                if c:
                    value = value + acc[p, :, lanes]
                acc[p, :, lanes] = value
                return 0

            return lax.fori_loop(0, GROUPS, rows, 0)

        lax.fori_loop(0, SHARE // 256, columns, 0)

    for at, copy in sends:
        if at == PARTS - 1:
            copy.wait_recv()
    backs = []
    own = None
    lanes_here = pl.ds(pl.multiple_of(me * SHARE, SHARE), SHARE)
    for d in (2, 1, 3, 0):
        p = peer(d)

        def columns(s, _, p=p):
            lanes = pl.ds(pl.multiple_of(s * 256, 256), 256)
            high, low = halves(recv_b[:, lanes])
            value = dot(w_hi_b[p], high) + dot(w_lo_b[p], high) + dot(w_hi_b[p], low)
            acc[p, :, lanes] = value + acc[p, :, lanes]
            return 0

        lax.fori_loop(0, SHARE // 256, columns, 0)
        if d:
            copy = pltpu.make_async_remote_copy(
                src_ref=acc.at[p, pl.ds(0, PADDED), :], dst_ref=mixed_ref.at[:, lanes_here],
                send_sem=back_send.at[d - 1], recv_sem=back_recv.at[d - 1],
                device_id=(block, p), device_id_type=MESH,
            )
            copy.start()
            backs.append(copy)
        else:
            own = pltpu.make_async_copy(acc.at[p, pl.ds(0, PADDED), :], mixed_ref.at[:, lanes_here], own_sem)
            own.start()

    for copy in sum_copies:
        copy.wait()
    whole = (sums[0] + sums[1]) + (sums[2] + sums[3])
    damp_ref[...] = 0.5 * whole / (1.0 + whole)
    for copy in stores:
        copy.wait()
    for _, copy in sends:
        copy.wait_send()
    own.wait()
    for copy in backs:
        copy.wait()


def finish_kernel(first_ref, moved_ref, mixed_ref, grow_ref, wind_ref, damp_ref, sea_ref, low_ref, place_ref, out_ref):
    tiles = moved_ref.shape[1] // 8

    def tile(j, _):
        at = pl.ds(pl.multiple_of(j * 8, 8), 8)
        grow = grow_ref[at, :]

        def one(i, row):
            first = first_ref[i]
            here = mixed_ref[at, pl.ds(pl.multiple_of(first * LAT, LAT), LAT)]
            after = jnp.minimum(first + 1, TILES - 1)
            there = mixed_ref[at, pl.ds(pl.multiple_of(after * LAT, LAT), LAT)]
            joined = jnp.where(low_ref[i] != 0, here, there)
            term = jnp.take_along_axis(joined, place_ref[i], axis=1)
            value = moved_ref[row, at, :]
            source = value * (grow * wind_ref[i] - damp_ref[i]) + term
            out_ref[row, at, :] = value + 0.5 * jnp.where(sea_ref[i] != 0.0, source, 0.0)

        def several(s, _):
            for u in range(4):
                i = s * 4 + u
                one(i, i + 1)
            return 0

        lax.fori_loop(0, (LON - 1) // 4, several, 0)
        one(LON - 1, 0)
        return 0

    lax.fori_loop(0, tiles, tile, 0)


def on_device(
    spectrum, sea_mask, cour_lon, cour_lat, wind, growth_rate, band_weight, freq_mix, dir_mix, routes, counts
):
    spec = jnp.transpose(spectrum, (1, 0, 2))
    sea, source, low, cross, last, first, place = tables(sea_mask)
    me = lax.axis_index("bin")
    own_weight = lax.dynamic_slice(band_weight, (me * LOCAL,), (LOCAL,))
    own_growth = lax.dynamic_slice(growth_rate, (me * LOCAL,), (LOCAL,))
    lanes = jnp.arange(LAT)[None, :]
    along_up = jnp.maximum(cour_lon, 0.0)
    along_down = jnp.minimum(cour_lon, 0.0)
    across_up = jnp.broadcast_to(jnp.maximum(cour_lat, 0.0)[:, None], cour_lon.shape)
    across_down = jnp.broadcast_to(jnp.minimum(cour_lat, 0.0)[:, None], cour_lon.shape)
    coef = jnp.stack([
        1.0 - along_up + along_down - across_up + across_down,
        along_up,
        -along_down,
        jnp.where(lanes == 0, 0.0, across_up),
        jnp.where(lanes == LAT - 1, 0.0, -across_down),
        jnp.broadcast_to(own_weight[:, None], cour_lon.shape),
    ])
    coef = jnp.pad(coef, ((0, 0), (0, PADDED - LOCAL), (0, 0)))
    fcol, dcol = column_maps()
    f32, bf16 = jnp.float32, jnp.bfloat16
    vmem = pl.BlockSpec(memory_space=pltpu.VMEM)
    hbm = pl.BlockSpec(memory_space=pl.ANY)
    smem = pl.BlockSpec(memory_space=pltpu.SMEM)
    dma = pltpu.SemaphoreType.DMA
    moved, mixed, damp = pl.pallas_call(
        exchange_kernel,
        out_shape=(
            jax.ShapeDtypeStruct((LON, LOCAL, LAT), f32),
            jax.ShapeDtypeStruct((PADDED, CELLS), f32),
            jax.ShapeDtypeStruct((LON, LAT), f32),
        ),
        in_specs=[smem, hbm] + [vmem] * 9,
        out_specs=(hbm, hbm, vmem),
        scratch_shapes=[
            pltpu.VMEM((LON, PADDED, LAT), f32),
            pltpu.VMEM((2, PADDED, LAT), f32),
            pltpu.VMEM((2, 8, LAT), f32),
            pltpu.VMEM((LON + 1, max(SIZES), LAT), f32),
            pltpu.VMEM((GROUPS - 1, PADDED, SHARE), f32),
            pltpu.VMEM((PARTS - 1, GROUPS * SIZES[0], SHARE), f32),
            pltpu.VMEM((GROUPS * SIZES[-1], SHARE), f32),
            pltpu.VMEM((GROUPS, MROWS, SHARE), f32),
            pltpu.VMEM((PARTS - 1, GROUPS, MROWS, GROUPS * SIZES[0]), bf16),
            pltpu.VMEM((PARTS - 1, GROUPS, MROWS, GROUPS * SIZES[0]), bf16),
            pltpu.VMEM((GROUPS, MROWS, GROUPS * SIZES[-1]), bf16),
            pltpu.VMEM((GROUPS, MROWS, GROUPS * SIZES[-1]), bf16),
            pltpu.VMEM((NF, KTOTAL), f32),
            pltpu.VMEM((4 * ND, KTOTAL), f32),
            pltpu.VMEM((LON, 8, LAT), f32),
            pltpu.VMEM((GROUPS, LON, LAT), f32),
            dma((PARTS,)), dma((PARTS,)), dma((4,)), dma((4,)), dma((PARTS, 3)), dma((PARTS, 3)),
            dma((3,)), dma((3,)), dma((3,)), dma((3,)), dma,
        ],
        compiler_params=pltpu.CompilerParams(
            collective_id=0, has_side_effects=True, vmem_limit_bytes=52 << 20
        ),
    )(last, spec, coef, sea, source, low, cross, freq_mix, dir_mix, jnp.asarray(fcol), jnp.asarray(dcol))

    def wide(a):
        return jnp.broadcast_to(jnp.roll(a, -1, axis=0)[:, None, :], (LON, 8, LAT))

    grow = jnp.broadcast_to(own_growth[:, None], (LOCAL, LAT))
    step = 56
    whole = pl.BlockSpec((LON, 8, LAT), lambda c: (0, 0, 0))
    damp_wide = jnp.broadcast_to(damp[:, None, :], (LON, 8, LAT))
    out = pl.pallas_call(
        finish_kernel,
        out_shape=jax.ShapeDtypeStruct((LON, LOCAL, LAT), f32),
        grid=(pl.cdiv(LOCAL, step),),
        in_specs=[
            smem,
            pl.BlockSpec((LON, step, LAT), lambda c: (0, c, 0)),
            pl.BlockSpec((step, CELLS), lambda c: (c, 0)),
            pl.BlockSpec((step, LAT), lambda c: (c, 0)),
            whole, whole, whole, whole, whole,
        ],
        out_specs=pl.BlockSpec((LON, step, LAT), lambda c: (0, c, 0)),
        compiler_params=pltpu.CompilerParams(vmem_limit_bytes=40 << 20),
    )(first, moved, mixed, grow, wide(wind), damp_wide, sea, low, place)
    return jnp.transpose(out, (1, 0, 2))


def solution(mesh):
    placed = (
        P("bin", "lon", None),
        P("lon", None),
        P("bin", None),
        P("bin"),
        P("lon", None),
        P(),
        P(),
        P(),
        P(),
        P("lon", None, None),
        P("lon", None),
    )
    return jax.shard_map(
        on_device, mesh=mesh, in_specs=placed, out_specs=P("bin", "lon", None), check_vma=False
    )
```

time: 435 us -> 202 us (0.46)
  Pallas kernels: 0 us -> 183 us
  waiting for transfers between devices: 158 us -> 0 us
  local copies, waits for them, and re-layouts: 147 us -> 10.6 us
  other arithmetic: 75.3 us -> 6.17 us
  starting transfers between devices: 28.4 us -> 0 us
  matrix products: 23.7 us -> 0.21 us
    pallas_call x0 -> x2, Pallas kernels: none -> 183 us  [the longest x1 137 us: on_device(): pl.pallas_call(exchange_kernel, out_shape=(jax.ShapeDtypeStruct((LON, LOC...]
    all_to_all x3 -> x0, waiting for transfers between devices: 158 us -> none  [the longest x1 79.2 us: on_device(): lax.all_to_all(sending, ('lon', 'bin'), split_axis=1, concat_axis=1, tile...]
    gather x2 -> x0, local copies, waits for them, and re-layouts: 43.6 us -> none  [the longest x1 23 us: on_device(): gust_send = wind_flat[slots].reshape(1, owners, capacity)]
    reshape x4 -> x0, local copies, waits for them, and re-layouts: 39.9 us -> none  [the longest x2 30.2 us: sources(): return full * factor + mixed.reshape(full.shape)]
    scatter-add x1 -> x0, other arithmetic: 29.4 us -> none  [on_device(): term = jnp.zeros((bins, cells), jnp.float32).at[:, slots].add(kept_terms)]
    all_to_all x3 -> x0, starting transfers between devices: 25.3 us -> none  [the longest x1 10.2 us: on_device(): lax.all_to_all(gust_send, ('lon', 'bin'), split_axis=1, concat_axis=1, ti...]
    dot_general x2 -> x1, matrix products: 23.7 us -> 0.21 us  [tables(): rank = jnp.dot(sea, upto).astype(jnp.int32)]
    mul x2 -> x0, other arithmetic: 20.9 us -> none  [the longest x1 17.2 us: on_device(): moved = advect(padded, cour_lon, cour_lat) * sea[None]]
  transfers between devices with their start and end apart: 5 -> 0, of which waited for: 2 -> 0; matrix products, arithmetic and copies ran while one was open for 19% -> 0% of each run, Pallas kernels for 0% -> 0%
where the time goes in v1:
time: 202 us; the launch traced here: 201 us
  Pallas kernels  183 us (91%)
  local copies, waits for them, and re-layouts  10.6 us (5%)
  other arithmetic  6.17 us (3%)
    pallas_call x1, Pallas kernels, on_device(): pl.pallas_call(exchange_kernel, out_shape=(jax.ShapeDtypeStruct((LON, LOC...  137 us
    pallas_call x1, Pallas kernels, on_device(): pl.pallas_call(finish_kernel, out_shape=jax.ShapeDtypeStruct((LON, LOCAL,...  46.3 us
    unnamed x12, local copies, waits for them, and re-layouts  5.68 us

profile of v1, /device:TPU:1, one launch (start us, length us, event | category | flops | bytes accessed | tf_op | source)
XLA Modules:
  0.0 200.7 jit_solution(4022829789703984685)
XLA Ops:
  0.0 0.0 copy-start.2
  0.0 0.0 copy-start.3
  0.0 0.0 copy-start.5
  0.0 0.0 copy-start.4
  0.0 0.7 slice.30
  0.8 0.8 dynamic_slice.7
  1.6 0.8 dynamic_slice.6
  2.3 0.7 fusion.8
  3.0 0.7 convert_element_type.45
  3.8 0.7 slice.29
  4.5 0.2 convolution_convert_fusion
  4.8 0.1 select_reduce_fusion
  4.9 0.2 convert_reduce_fusion.1
  5.1 0.1 copy.16
  5.2 0.1 copy.20
  5.3 0.1 add_select_fusion
  5.4 0.1 copy.21
  5.5 0.1 copy.17
  5.6 1.1 convert_reduce_fusion
  6.7 0.1 copy.18
  6.8 0.1 copy.19
  7.0 0.1 broadcast_in_dim.50.grow_ref
  7.1 0.1 broadcast_in_dim_broadcast_in_dim_broadcast_in_dim.2.cross_ref
  7.2 1.1 bitcast_dynamic-update-slice_fusion.2
  8.3 0.9 bitcast_dynamic-update-slice_fusion.1
  9.2 0.9 bitcast_dynamic-update-slice_fusion
  10.2 0.1 select_dynamic-update-slice_fusion.1
  10.3 0.1 select_dynamic-update-slice_fusion
  10.4 0.1 broadcast_dynamic-update-slice_fusion
  10.5 1.0 pad.4.coef_ref
  11.5 0.0 copy-done.2
  11.5 0.0 copy-done.3
  11.5 0.0 copy-done.5
  11.5 0.0 copy-done.4
  11.5 137.2 %shard_map.109 = (f32[45,324,128]{2,1,0:T(8,128)}, f32[328,4096]{1,0:T(8,128)}, f32[45,128]{1,0:T(8,128)S(1)}) custom-call(s32[32]{0:T(128)S(1)} %broadcast_add_fusion.last_ref, f32[45,324,128]{2,1,0:T(8,128)} %bitcast.18, f32[6,328,128]{2,1,0:T(8,128)} %pad.4.coef_ref, f32[45,8,128]{2,1,0:T(8,128)S(1)} %broadcast_in_dim.42.sea_ref, ...), custom_call_target="tpu_custom_call" | custom-call | tf_op jit(solution)/shard_map/pallas_call | solution.py:391
  148.7 0.0 copy-start
  148.8 3.1 %copy-done = f32[45,324,128]{2,1,0:T(8,128)S(1)} copy-done((f32[45,324,128]{2,1,0:T(8,128)S(1)}, f32[45,324,128]{2,1,0:T(8,128)}, u32[]{:S(2)}) %copy-start) | copy-done | bytes 7464984
  151.9 0.0 copy-start.1
  151.9 2.5 %copy-done.1 = f32[328,4096]{1,0:T(8,128)S(1)} copy-done((f32[328,4096]{1,0:T(8,128)S(1)}, f32[328,4096]{1,0:T(8,128)}, u32[]{:S(2)}) %copy-start.1) | copy-done | bytes 5373976
  154.4 46.3 %shard_map.110 = f32[45,324,128]{2,1,0:T(8,128)} custom-call(s32[45]{0:T(128)S(1)} %fusion.7.first_ref, f32[45,324,128]{2,1,0:T(8,128)S(1)} %copy-done, f32[328,4096]{1,0:T(8,128)S(1)} %copy-done.1, f32[324,128]{1,0:T(8,128)S(1)} %broadcast_in_dim.50.grow_ref, f32[45,8,128]{2,1,0:T(8,128)S(1)} %broadcast_in_dim.51.wind_ref, ...), custom_call_target="tpu_custom_call" | custom-call | tf_op jit(solution)/shard_map/pallas_call | solution.py:432
  (21 shorter events, 0.2 us)
Async XLA Ops:
  0.0 11.5 %copy-start.2 = (f32[36,1312]{1,0:T(8,128)S(1)}, f32[36,1312]{1,0:T(8,128)}, u32[]{:S(2)}) copy-start(f32[36,1312]{1,0:T(8,128)} %constant.76.clone.dcol_ref) | copy-start | bytes 566788
  0.0 11.5 %copy-start.3 = (f32[36,1312]{1,0:T(8,128)S(1)}, f32[36,1312]{1,0:T(8,128)}, u32[]{:S(2)}) copy-start(f32[36,1312]{1,0:T(8,128)} %constant.75.clone.fcol_ref) | copy-start | bytes 566788
  0.0 11.5 %copy-start.5 = (f32[36,36]{1,0:T(8,128)S(1)}, f32[36,36]{1,0:T(8,128)}, u32[]{:S(2)}) copy-start(f32[36,36]{1,0:T(8,128)} %dmix_ref.1) | copy-start | bytes 15556
  0.0 11.5 %copy-start.4 = (f32[36,36]{1,0:T(8,128)S(1)}, f32[36,36]{1,0:T(8,128)}, u32[]{:S(2)}) copy-start(f32[36,36]{1,0:T(8,128)} %fmix_ref.1) | copy-start | bytes 15556
  148.7 3.1 %copy-start = (f32[45,324,128]{2,1,0:T(8,128)S(1)}, f32[45,324,128]{2,1,0:T(8,128)}, u32[]{:S(2)}) copy-start(f32[45,324,128]{2,1,0:T(8,128)} %get-tuple-element.8.moved_ref) | copy-start | bytes 22394884
  151.9 2.5 %copy-start.1 = (f32[328,4096]{1,0:T(8,128)S(1)}, f32[328,4096]{1,0:T(8,128)}, u32[]{:S(2)}) copy-start(f32[328,4096]{1,0:T(8,128)} %get-tuple-element.9.mixed_ref) | copy-start | bytes 16121860

commit v2 on v1

v2 whole, which is shorter than its diff:
```python
import functools

import jax
import jax.numpy as jnp
import numpy as np
from jax import lax
from jax.experimental import pallas as pl
from jax.experimental.pallas import tpu as pltpu
from jax.sharding import PartitionSpec as P

MESH = pl.DeviceIdType.MESH
NF, ND = 36, 36
LON, LAT = 45, 128
GROUPS = 4
LOCAL = 324
PADDED = 328
CELLS = 4096
SHARE = CELLS // GROUPS
TILES = CELLS // LAT
SIZES = (64, 64, 64, 64, 72)
STARTS = (0, 64, 128, 192, 256)
PARTS = len(SIZES)
KSTARTS = tuple(GROUPS * s for s in STARTS)
KTOTAL = GROUPS * PADDED
MROWS = 336
ROWS_AT_ONCE = 10


def column_maps():
    freq = np.zeros((NF, KTOTAL), np.float32)
    direction = np.zeros((ND, KTOTAL), np.float32)
    at = 0
    for start, size in zip(STARTS, SIZES):
        for p in range(GROUPS):
            for b in range(start, start + size):
                if b < LOCAL:
                    k = p * LOCAL + b
                    freq[k // ND, at] = 1.0
                    direction[k % ND, at] = 1.0
                at += 1
    return freq, direction


def exchange_kernel(
    spec_ref, mask_ref, cour_ref, lat_ref, wind_ref, growth_ref, weight_ref, fmix_ref, dmix_ref, fcol_ref, dcol_ref,
    moved_ref, mixed_ref, damp_ref, gust_ref, live_ref, low_ref, place_ref, first_ref, grow_ref,
    x, moved, sea, source, cross, order, last_rows, last, coef, packed, stage, recv_a, recv_b, acc,
    w_hi_a, w_lo_a, w_hi_b, w_lo_b, fcols, dcols, steep, sums,
    in_sem, out_sem, halo_send, halo_recv, send_sem, recv_sem, back_send, back_recv, sum_send, sum_recv, own_sem, last_sem,
):
    me = lax.axis_index("bin")
    block = lax.axis_index("lon")
    blocks = lax.axis_size("lon")
    west = lax.rem(block + blocks - 1, blocks)
    east = lax.rem(block + 1, blocks)

    def peer(d):
        return lax.rem(me + d, GROUPS)

    barrier = pltpu.get_barrier_semaphore()
    for d in (1, 2, 3):
        pl.semaphore_signal(barrier, inc=1, device_id=(block, peer(d)), device_id_type=MESH)
    pl.semaphore_signal(barrier, inc=1, device_id=(west, me), device_id_type=MESH)
    pl.semaphore_signal(barrier, inc=1, device_id=(east, me), device_id_type=MESH)

    loads = []
    for c in range(PARTS):
        rows = min(SIZES[c], LOCAL - STARTS[c])
        copy = pltpu.make_async_copy(
            spec_ref.at[:, pl.ds(STARTS[c], rows), :],
            x.at[pl.ds(1, LON), pl.ds(STARTS[c], rows), :],
            in_sem.at[c],
        )
        copy.start()
        loads.append(copy)

    flags = mask_ref[...].astype(jnp.float32)
    for r in range(LON):
        wide = jnp.broadcast_to(flags[r:r + 1, :], (8, LAT))
        sea[r + 1] = wide
        live_ref[(r - 1) % LON] = wide
    order[pl.ds(0, LON - 1), :] = flags[1:, :]
    order[pl.ds(LON - 1, 1), :] = flags[:1, :]
    order[pl.ds(LON, 3), :] = jnp.zeros((3, LAT), jnp.float32)

    pl.semaphore_wait(barrier, 5)
    edges = []
    for slot, row, into, to in ((0, LON - 1, 0, east), (1, 0, LON + 1, west)):
        copy = pltpu.make_async_remote_copy(
            src_ref=spec_ref.at[row], dst_ref=x.at[into, pl.ds(0, LOCAL), :],
            send_sem=halo_send.at[slot], recv_sem=halo_recv.at[slot], device_id=(to, me), device_id_type=MESH,
        )
        copy.start()
        edges.append(copy)
        copy = pltpu.make_async_remote_copy(
            src_ref=sea.at[row + 1], dst_ref=sea.at[into],
            send_sem=halo_send.at[2 + slot], recv_sem=halo_recv.at[2 + slot], device_id=(to, me), device_id_type=MESH,
        )
        copy.start()
        edges.append(copy)

    dot = functools.partial(jnp.dot, preferred_element_type=jnp.float32)
    steps = LON + 3
    here = order[...]
    down = lax.broadcasted_iota(jnp.int32, (LAT, LAT), 0)
    across = lax.broadcasted_iota(jnp.int32, (LAT, LAT), 1)
    rank = dot(here, (down <= across).astype(jnp.float32))
    number = dot(here, jnp.ones((LAT, LAT), jnp.float32))
    before = lax.broadcasted_iota(jnp.int32, (steps, steps), 0) > lax.broadcasted_iota(jnp.int32, (steps, steps), 1)
    offset = dot(before.astype(jnp.float32), number).astype(jnp.int32)
    lane = lax.broadcasted_iota(jnp.int32, (steps, LAT), 1)
    step_of = lax.broadcasted_iota(jnp.int32, (steps, LAT), 0)
    reached = jnp.where((offset <= lane * LAT + (LAT - 1)) & (step_of <= LON), 1, 0)
    last_rows[...] = jnp.broadcast_to(jnp.sum(reached, axis=0, keepdims=True) - 1, (8, LAT))
    copy_last = pltpu.make_async_copy(last_rows, last, last_sem)
    copy_last.start()
    first_ref[...] = jnp.minimum(offset // LAT, TILES - 1)
    shift = offset % LAT
    for t in range(steps // 8):
        some = slice(8 * t, 8 * t + 8)
        ranks, moved_by = rank[some], shift[some]
        lanes = lane[some]
        wanted = ((lanes - moved_by + LAT) % LAT).astype(jnp.float32)
        position = jnp.zeros((8, LAT), jnp.int32)
        for half in (64, 32, 16, 8, 4, 2, 1):
            probe = jnp.take_along_axis(ranks, position + (half - 1), axis=1)
            position = jnp.where(probe <= wanted, position + half, position)
        low = (lanes >= moved_by).astype(jnp.int32)
        over = (moved_by.astype(jnp.float32) + number[some] >= LAT).astype(jnp.int32)
        place = (moved_by + ranks.astype(jnp.int32) + (LAT - 1)) % LAT
        for u in range(8):
            i = 8 * t + u
            if i < LON:
                for ref, value in ((source, position), (low_ref, low), (cross, over), (place_ref, place)):
                    ref[i] = jnp.broadcast_to(value[u:u + 1, :], (8, LAT))
                gust_ref[i] = jnp.broadcast_to(wind_ref[(i + 1) % LON:(i + 1) % LON + 1, :], (8, LAT))

    def own(ref):
        part = [ref[:, LOCAL * p:LOCAL * (p + 1)] for p in range(GROUPS)]
        return jnp.where(me < 2, jnp.where(me == 0, part[0], part[1]), jnp.where(me == 2, part[2], part[3]))

    def columns_of(row):
        row = jnp.concatenate([row, jnp.zeros((1, 3 * LAT - LOCAL), jnp.float32)], axis=1)
        return [jnp.broadcast_to(row[:, LAT * b:LAT * (b + 1)], (LAT, LAT)).T for b in range(3)]

    at_lat, at_weight, at_growth = columns_of(lat_ref[...]), columns_of(own(weight_ref)), columns_of(own(growth_ref))
    for b in range(3):
        rows = min(LAT, PADDED - LAT * b)
        real = min(LAT, LOCAL - LAT * b)
        to = pl.ds(LAT * b, rows)
        along = cour_ref[pl.ds(LAT * b, real), :]
        if real < rows:
            along = jnp.concatenate([along, jnp.zeros((rows - real, LAT), jnp.float32)], axis=0)
        up, down_by = jnp.maximum(along, 0.0), jnp.minimum(along, 0.0)
        lat = at_lat[b][:rows]
        north, south = jnp.maximum(lat, 0.0), jnp.minimum(lat, 0.0)
        lanes = lax.broadcasted_iota(jnp.int32, (rows, LAT), 1)
        coef[0, to, :] = 1.0 - up + down_by - north + south
        coef[1, to, :] = up
        coef[2, to, :] = -down_by
        coef[3, to, :] = jnp.where(lanes == 0, 0.0, north)
        coef[4, to, :] = jnp.where(lanes == LAT - 1, 0.0, -south)
        coef[5, to, :] = at_weight[b][:rows]
        grow_ref[to, :] = at_growth[b][:rows]

    steep[...] = jnp.zeros_like(steep)
    pad = PADDED - LOCAL
    x[:, pl.ds(LOCAL, pad), :] = jnp.zeros((LON + 2, pad, LAT), jnp.float32)

    def group_of(start, n, base, part):
        at = [pl.ds(pl.multiple_of(base + 8 * j, 8), 8) for j in range(n)]
        to = [pl.ds(pl.multiple_of(base - start + 8 * j, 8), 8) for j in range(n)]
        coefs = [[coef[q, at[j], :] for q in range(6)] for j in range(n)]

        def masked(row, j):
            return x[row, at[j], :] * sea[row]

        def treat(todo, sides, hold):
            stores = []
            for i, row, fresh in todo:
                land, turn, low, over, total = sea[row], source[i], low_ref[i] != 0, cross[i] != 0, steep[i]
                if fresh:
                    sides = [(masked(row - 1, j), masked(row, j)) for j in range(n)]
                new_hold = []
                for j in range(n):
                    c0, cw, ce, cs, cn, weight = coefs[j]
                    low_side, mid = sides[j]
                    high_side = masked(row + 1, j)
                    value = c0 * mid + cw * low_side + ce * high_side
                    value = value + cs * pltpu.roll(mid, 1, 1) + cn * pltpu.roll(mid, LAT - 1, 1)
                    value = value * land
                    total = total + weight * value
                    turned = jnp.take_along_axis(value, turn, axis=1)
                    kept = jnp.where(low, turned, hold[j])
                    stores.append((moved, row - 1, at[j], value))
                    stores.append((packed, i, to[j], kept))
                    new_hold.append(jnp.where(over, turned, kept))
                    sides[j] = (mid, high_side)
                stores.append((steep, i, slice(None), total))
                hold = new_hold
            for ref, i, rows, value in stores:
                ref[i, rows, :] = value
            return sides, hold

        if part != 1:
            sides = [(masked(1, j), masked(2, j)) for j in range(n)]
            hold = [jnp.zeros((8, LAT), jnp.float32) for j in range(n)]

            def several(s, carry):
                sides, hold = treat(
                    [(s * ROWS_AT_ONCE + u, s * ROWS_AT_ONCE + u + 2, False) for u in range(ROWS_AT_ONCE)],
                    list(carry[0]), list(carry[1]),
                )
                return (tuple(sides), tuple(hold))

            inner = LON - 2
            count = inner // ROWS_AT_ONCE
            sides, hold = lax.fori_loop(0, count, several, (tuple(sides), tuple(hold)))
            sides, hold = list(sides), list(hold)
            rest = [(i, i + 2, False) for i in range(count * ROWS_AT_ONCE, inner)]
        else:
            sides, rest = None, []
            hold = [packed[LON, to[j], :] for j in range(n)]
        if part != 0:
            rest = rest + [(LON - 2, LON, part == 1), (LON - 1, 1, True)]
        if rest:
            sides, hold = treat(rest, sides, hold)
        for j in range(n):
            packed[LON, to[j], :] = hold[j]

    sends = []
    stores = []
    for c in range(PARTS):
        start, size = STARTS[c], SIZES[c]
        n = 2 if size % 16 == 0 else 3
        loads[c].wait()
        for part in ((0, 1) if c == 0 else (None,)):
            if part == 1:
                for copy in edges:
                    copy.wait()

            def group(s, _, start=start, n=n, part=part):
                group_of(start, n, start + s * 8 * n, part)
                return 0

            lax.fori_loop(0, size // (8 * n), group, 0)
        rows = min(size, LOCAL - start)
        copy = pltpu.make_async_copy(
            moved.at[:, pl.ds(start, rows), :], moved_ref.at[:, pl.ds(start, rows), :], out_sem.at[c]
        )
        copy.start()
        stores.append(copy)
        if c == 0:
            copy_last.wait()
        recv = recv_b if c == PARTS - 1 else recv_a.at[c]
        mine = pl.ds(pl.multiple_of(me * size, 8), size)
        for d in (2, 1, 3, 0):
            to = peer(d)
            values = [
                packed[last[0, to * (SHARE // LAT) + k], pl.ds(0, size), :] for k in range(SHARE // LAT)
            ]
            for k in range(SHARE // LAT):
                lanes = pl.ds(k * LAT, LAT)
                if d == 0:
                    recv[mine, lanes] = values[k]
                else:
                    stage[d - 1, pl.ds(start, size), lanes] = values[k]
            if d:
                copy = pltpu.make_async_remote_copy(
                    src_ref=stage.at[d - 1, pl.ds(start, size), :], dst_ref=recv.at[mine, :],
                    send_sem=send_sem.at[c, d - 1], recv_sem=recv_sem.at[c, d - 1],
                    device_id=(block, to), device_id_type=MESH,
                )
                copy.start()
                sends.append((c, copy))

    sums[0] = jnp.sum(steep[...], axis=1)
    sum_copies = []
    for d in (1, 2, 3):
        copy = pltpu.make_async_remote_copy(
            src_ref=sums.at[0], dst_ref=sums.at[d], send_sem=sum_send.at[d - 1], recv_sem=sum_recv.at[d - 1],
            device_id=(block, peer(d)), device_id_type=MESH,
        )
        copy.start()
        sum_copies.append(copy)

    exact = functools.partial(jnp.dot, precision=lax.Precision.HIGHEST, preferred_element_type=jnp.float32)
    fcols[...] = exact(fmix_ref[...], fcol_ref[...])
    spread = exact(dmix_ref[...], dcol_ref[...])
    for j in range(4):
        dcols[pl.ds(j * ND, ND), :] = spread

    def matrix_rows(p, _):
        for g, (size, count) in enumerate(((144, 4), (144, 4), (48, 1))):
            for c in range(PARTS):
                width = GROUPS * SIZES[c]
                cols = pl.ds(KSTARTS[c], width)
                index = lax.broadcasted_iota(jnp.int32, (size, width), 0)
                rows = [fcols[pl.ds(p * 9 + 4 * g + j, 1), cols] for j in range(count)]
                if count == 1:
                    factor = jnp.where(index < ND, rows[0], 0.0)
                else:
                    factor = jnp.where(
                        index < 2 * ND,
                        jnp.where(index < ND, rows[0], rows[1]),
                        jnp.where(index < 3 * ND, rows[2], rows[3]),
                    )
                value = factor * dcols[pl.ds(0, size), cols]
                high = value.astype(jnp.bfloat16)
                low = (value - high.astype(jnp.float32)).astype(jnp.bfloat16)
                at = pl.ds(144 * g, size)
                if c == PARTS - 1:
                    w_hi_b[p, at, :] = high
                    w_lo_b[p, at, :] = low
                else:
                    w_hi_a[c, p, at, :] = high
                    w_lo_a[c, p, at, :] = low
        return 0

    lax.fori_loop(0, GROUPS, matrix_rows, 0)

    def halves(value):
        high = value.astype(jnp.bfloat16)
        return high, (value - high.astype(jnp.float32)).astype(jnp.bfloat16)

    for c in range(PARTS - 1):
        for at, copy in sends:
            if at == c:
                copy.wait_recv()

        def columns(s, _, c=c):
            lanes = pl.ds(pl.multiple_of(s * 256, 256), 256)
            high, low = halves(recv_a[c, :, lanes])

            def rows(p, _):
                value = dot(w_hi_a[c, p], high) + dot(w_lo_a[c, p], high) + dot(w_hi_a[c, p], low)
                if c:
                    value = value + acc[p, :, lanes]
                acc[p, :, lanes] = value
                return 0

            return lax.fori_loop(0, GROUPS, rows, 0)

        lax.fori_loop(0, SHARE // 256, columns, 0)

    for at, copy in sends:
        if at == PARTS - 1:
            copy.wait_recv()
    backs = []
    own_copy = None
    lanes_here = pl.ds(pl.multiple_of(me * SHARE, SHARE), SHARE)
    for d in (2, 1, 3, 0):
        p = peer(d)

        def columns(s, _, p=p):
            lanes = pl.ds(pl.multiple_of(s * 256, 256), 256)
            high, low = halves(recv_b[:, lanes])
            value = dot(w_hi_b[p], high) + dot(w_lo_b[p], high) + dot(w_hi_b[p], low)
            acc[p, :, lanes] = value + acc[p, :, lanes]
            return 0

        lax.fori_loop(0, SHARE // 256, columns, 0)
        if d:
            copy = pltpu.make_async_remote_copy(
                src_ref=acc.at[p, pl.ds(0, PADDED), :], dst_ref=mixed_ref.at[:, lanes_here],
                send_sem=back_send.at[d - 1], recv_sem=back_recv.at[d - 1],
                device_id=(block, p), device_id_type=MESH,
            )
            copy.start()
            backs.append(copy)
        else:
            own_copy = pltpu.make_async_copy(acc.at[p, pl.ds(0, PADDED), :], mixed_ref.at[:, lanes_here], own_sem)
            own_copy.start()

    for copy in sum_copies:
        copy.wait()
    whole = (sums[0] + sums[1]) + (sums[2] + sums[3])
    whole = 0.5 * whole / (1.0 + whole)
    for i in range(LON):
        damp_ref[i] = jnp.broadcast_to(whole[i:i + 1, :], (8, LAT))
    for copy in stores:
        copy.wait()
    for _, copy in sends:
        copy.wait_send()
    own_copy.wait()
    for copy in backs:
        copy.wait()


def finish_kernel(first_ref, moved_ref, mixed_ref, grow_ref, gust_ref, damp_ref, live_ref, low_ref, place_ref, out_ref):
    tiles = moved_ref.shape[1] // 8

    def treat(todo):
        stores = []
        for i, row in todo:
            first = first_ref[i, 0]
            here = pl.ds(pl.multiple_of(first * LAT, LAT), LAT)
            there = pl.ds(pl.multiple_of(jnp.minimum(first + 1, TILES - 1) * LAT, LAT), LAT)
            low, place, gust, damp, live = low_ref[i] != 0, place_ref[i], gust_ref[i], damp_ref[i], live_ref[i] != 0.0
            for j in range(tiles):
                at = pl.ds(8 * j, 8)
                joined = jnp.where(low, mixed_ref[at, here], mixed_ref[at, there])
                term = jnp.take_along_axis(joined, place, axis=1)
                value = moved_ref[row, at, :]
                source = value * (grow_ref[at, :] * gust - damp) + term
                stores.append((row, at, value + jnp.where(live, 0.5 * source, 0.0)))
        for row, at, value in stores:
            out_ref[row, at, :] = value

    def several(s, _):
        treat([(s * 4 + u, s * 4 + u + 1) for u in range(4)])
        return 0

    lax.fori_loop(0, (LON - 1) // 4, several, 0)
    treat([(LON - 1, 0)])


def on_device(
    spectrum, sea_mask, cour_lon, cour_lat, wind, growth_rate, band_weight, freq_mix, dir_mix, routes, counts
):
    spec = jnp.transpose(spectrum, (1, 0, 2))
    fcol, dcol = column_maps()
    f32, bf16, i32 = jnp.float32, jnp.bfloat16, jnp.int32
    vmem = pl.BlockSpec(memory_space=pltpu.VMEM)
    hbm = pl.BlockSpec(memory_space=pl.ANY)
    smem = pl.BlockSpec(memory_space=pltpu.SMEM)
    dma = pltpu.SemaphoreType.DMA
    wide = (LON, 8, LAT)
    moved, mixed, damp, gust, live, low, place, first, grow = pl.pallas_call(
        exchange_kernel,
        out_shape=(
            jax.ShapeDtypeStruct((LON, LOCAL, LAT), f32),
            jax.ShapeDtypeStruct((PADDED, CELLS), f32),
            jax.ShapeDtypeStruct(wide, f32),
            jax.ShapeDtypeStruct(wide, f32),
            jax.ShapeDtypeStruct(wide, f32),
            jax.ShapeDtypeStruct(wide, i32),
            jax.ShapeDtypeStruct(wide, i32),
            jax.ShapeDtypeStruct((LON + 3, LAT), i32),
            jax.ShapeDtypeStruct((PADDED, LAT), f32),
        ),
        in_specs=[hbm] + [vmem] * 10,
        out_specs=(hbm, hbm) + (vmem,) * 7,
        scratch_shapes=[
            pltpu.VMEM((LON + 2, PADDED, LAT), f32),
            pltpu.VMEM((LON, PADDED, LAT), f32),
            pltpu.VMEM((LON + 2, 8, LAT), f32),
            pltpu.VMEM(wide, i32),
            pltpu.VMEM(wide, i32),
            pltpu.VMEM((LON + 3, LAT), f32),
            pltpu.VMEM((8, LAT), i32),
            pltpu.SMEM((8, LAT), i32),
            pltpu.VMEM((6, PADDED, LAT), f32),
            pltpu.VMEM((LON + 1, max(SIZES), LAT), f32),
            pltpu.VMEM((GROUPS - 1, PADDED, SHARE), f32),
            pltpu.VMEM((PARTS - 1, GROUPS * SIZES[0], SHARE), f32),
            pltpu.VMEM((GROUPS * SIZES[-1], SHARE), f32),
            pltpu.VMEM((GROUPS, MROWS, SHARE), f32),
            pltpu.VMEM((PARTS - 1, GROUPS, MROWS, GROUPS * SIZES[0]), bf16),
            pltpu.VMEM((PARTS - 1, GROUPS, MROWS, GROUPS * SIZES[0]), bf16),
            pltpu.VMEM((GROUPS, MROWS, GROUPS * SIZES[-1]), bf16),
            pltpu.VMEM((GROUPS, MROWS, GROUPS * SIZES[-1]), bf16),
            pltpu.VMEM((NF, KTOTAL), f32),
            pltpu.VMEM((4 * ND, KTOTAL), f32),
            pltpu.VMEM(wide, f32),
            pltpu.VMEM((GROUPS, LON, LAT), f32),
            dma((PARTS,)), dma((PARTS,)), dma((4,)), dma((4,)), dma((PARTS, 3)), dma((PARTS, 3)),
            dma((3,)), dma((3,)), dma((3,)), dma((3,)), dma, dma,
        ],
        compiler_params=pltpu.CompilerParams(
            collective_id=0, has_side_effects=True, vmem_limit_bytes=56 << 20
        ),
    )(
        spec, sea_mask, cour_lon, cour_lat.reshape(1, LOCAL), wind,
        growth_rate.reshape(1, -1), band_weight.reshape(1, -1), freq_mix, dir_mix, jnp.asarray(fcol), jnp.asarray(dcol),
    )
    step = 88
    whole = pl.BlockSpec(wide, lambda c: (0, 0, 0))
    out = pl.pallas_call(
        finish_kernel,
        out_shape=jax.ShapeDtypeStruct((LON, LOCAL, LAT), f32),
        grid=(pl.cdiv(LOCAL, step),),
        in_specs=[
            smem,
            pl.BlockSpec((LON, step, LAT), lambda c: (0, c, 0)),
            pl.BlockSpec((step, CELLS), lambda c: (c, 0)),
            pl.BlockSpec((step, LAT), lambda c: (c, 0)),
            whole, whole, whole, whole, whole,
        ],
        out_specs=pl.BlockSpec((LON, step, LAT), lambda c: (0, c, 0)),
        compiler_params=pltpu.CompilerParams(vmem_limit_bytes=58 << 20),
    )(first, moved, mixed, grow, gust, damp, live, low, place)
    return jnp.transpose(out, (1, 0, 2))


def solution(mesh):
    placed = (
        P("bin", "lon", None),
        P("lon", None),
        P("bin", None),
        P("bin"),
        P("lon", None),
        P(),
        P(),
        P(),
        P(),
        P("lon", None, None),
        P("lon", None),
    )
    return jax.shard_map(
        on_device, mesh=mesh, in_specs=placed, out_specs=P("bin", "lon", None), check_vma=False
    )
```

time: 202 us -> 149 us (0.74)
  Pallas kernels: 183 us -> 145 us
  local copies, waits for them, and re-layouts: 10.6 us -> 3.84 us
  other arithmetic: 6.17 us -> 0 us
    pallas_call x1, Pallas kernels: 46.3 us -> 11.2 us  [on_device(): pl.pallas_call(finish_kernel, out_shape=jax.ShapeDtypeStruct((LON, LOCAL,...]
    unnamed x12 -> x0, local copies, waits for them, and re-layouts: 5.68 us -> none
    reshape x0 -> x3, local copies, waits for them, and re-layouts: none -> 3.84 us  [the longest x1 1.3 us: on_device(): band_weight.reshape(1, -1)]
    pallas_call x1, Pallas kernels: 137 us -> 133 us  [on_device(): pl.pallas_call(exchange_kernel, out_shape=(jax.ShapeDtypeStruct((LON, LOC...]
    unnamed x5 -> x0, other arithmetic: 3.15 us -> none
where the time goes in v2:
time: 149 us
  Pallas kernels  145 us (97%)
  local copies, waits for them, and re-layouts  3.84 us (3%)
    pallas_call x1, Pallas kernels, on_device(): pl.pallas_call(exchange_kernel, out_shape=(jax.ShapeDtypeStruct((LON, LOC...  133 us
    pallas_call x1, Pallas kernels, on_device(): pl.pallas_call(finish_kernel, out_shape=jax.ShapeDtypeStruct((LON, LOCAL,...  11.2 us

profile of v2, /device:TPU:1, one launch (start us, length us, event | category | flops | bytes accessed | tf_op | source)
XLA Modules:
  0.0 148.5 jit_solution(12495998169373432645)
XLA Ops:
  0.0 1.3 reshape.9.lat_ref
  1.3 1.3 reshape.10.growth_ref
  2.5 1.3 reshape.11.weight_ref
  3.8 133.4 %shard_map.109 = (f32[45,324,128]{2,1,0:T(8,128)}, f32[328,4096]{1,0:T(8,128)}, f32[45,8,128]{2,1,0:T(8,128)}, f32[45,8,128]{2,1,0:T(8,128)}, f32[45,8,128]{2,1,...) custom-call(f32[45,324,128]{2,1,0:T(8,128)} %bitcast.2, ...), custom_call_target="tpu_custom_call" | custom-call | tf_op jit(solution)/shard_map/pallas_call | solution.py:429
  137.3 11.2 %shard_map.110 = f32[45,324,128]{2,1,0:T(8,128)} custom-call(s32[48,128]{1,0:T(8,128)} %get-tuple-element.14.first_ref, f32[45,324,128]{2,1,0:T(8,128)} %get-tuple-element.15.moved_ref, f32[328,4096]{1,0:T(8,128)} %get-tuple-element.16.mixed_ref, f32[328,128]{1,0:T(8,128)} %get-tuple-element.17.grow_ref, f32[45,8,128]{2,1,0:T(8,128)} %get-tuple-element.18.gust_ref, ...), custom_call_target="tpu_custom_call" | custom-call | tf_op jit(solution)/shard_map/pallas_call | solution.py:479

commit v3 on v2

v3 whole, which is shorter than its diff:
```python
import functools

import jax
import jax.numpy as jnp
import numpy as np
from jax import lax
from jax.experimental import pallas as pl
from jax.experimental.pallas import tpu as pltpu
from jax.sharding import PartitionSpec as P

MESH = pl.DeviceIdType.MESH
dissipation = 0.5
time_step = 0.5
NF, ND = 36, 36
LON, LAT = 45, 128
GROUPS = 4
LOCAL = 324
PADDED = 328
CELLS = 4096
SHARE = CELLS // GROUPS
TILES = CELLS // LAT
SIZES = (64, 64, 64, 64, 72)
STARTS = (0, 64, 128, 192, 256)
PARTS = len(SIZES)
KSTARTS = tuple(GROUPS * s for s in STARTS)
KTOTAL = GROUPS * PADDED
MROWS = 336
OWN = SHARE // LAT
HALF = OWN // 2
ROWS_AT_ONCE = 10


def column_maps():
    freq = np.zeros((NF, KTOTAL), np.float32)
    direction = np.zeros((ND, KTOTAL), np.float32)
    at = 0
    for start, size in zip(STARTS, SIZES):
        for p in range(GROUPS):
            for b in range(start, start + size):
                if b < LOCAL:
                    k = p * LOCAL + b
                    freq[k // ND, at] = 1.0
                    direction[k % ND, at] = 1.0
                at += 1
    return freq, direction


def exchange_kernel(
    spec_ref, mask_ref, cour_ref, wind_ref, bins_ref, fmix_ref, dmix_ref, fcol_ref, dcol_ref,
    moved_ref, mixed_ref, live_ref, low_ref, place_ref, first_ref,
    x, moved, sea, gust, damp, source, cross, head, order, last_rows, last, coef, grow, packed, edge, stage, recv, tail, acc,
    w_hi, w_lo, f_hi, f_lo, fcols, dcols, steep, sums,
    in_sem, halo_send, halo_recv, send_sem, recv_sem, back_send, back_recv, sum_send, sum_recv, own_sem, last_sem, out_sem,
):
    me = lax.axis_index("bin")
    block = lax.axis_index("lon")
    blocks = lax.axis_size("lon")
    west = lax.rem(block + blocks - 1, blocks)
    east = lax.rem(block + 1, blocks)

    def peer(d):
        return lax.rem(me + d, GROUPS)

    barrier = pltpu.get_barrier_semaphore()
    for d in (1, 2, 3):
        pl.semaphore_signal(barrier, inc=1, device_id=(block, peer(d)), device_id_type=MESH)
    pl.semaphore_signal(barrier, inc=1, device_id=(west, me), device_id_type=MESH)
    pl.semaphore_signal(barrier, inc=1, device_id=(east, me), device_id_type=MESH)

    loads = []
    for c in range(PARTS):
        rows = min(SIZES[c], LOCAL - STARTS[c])
        copy = pltpu.make_async_copy(
            spec_ref.at[:, pl.ds(STARTS[c], rows), :],
            x.at[pl.ds(1, LON), pl.ds(STARTS[c], rows), :],
            in_sem.at[c],
        )
        copy.start()
        loads.append(copy)

    flags = mask_ref[...].astype(jnp.float32)
    for r in range(LON):
        wide = jnp.broadcast_to(flags[r:r + 1, :], (8, LAT))
        sea[r + 1] = wide
        live_ref[(r + 1) % LON] = wide
    order[pl.ds(0, 1), :] = flags[LON - 1:, :]
    order[pl.ds(1, LON - 1), :] = flags[:LON - 1, :]
    order[pl.ds(LON, 3), :] = jnp.zeros((3, LAT), jnp.float32)

    dot = functools.partial(jnp.dot, preferred_element_type=jnp.float32)
    steps = LON + 3
    here = order[...]
    down = lax.broadcasted_iota(jnp.int32, (LAT, LAT), 0)
    across = lax.broadcasted_iota(jnp.int32, (LAT, LAT), 1)
    rank = dot(here, (down <= across).astype(jnp.float32))
    number = dot(here, jnp.ones((LAT, LAT), jnp.float32))
    before = lax.broadcasted_iota(jnp.int32, (steps, steps), 0) > lax.broadcasted_iota(jnp.int32, (steps, steps), 1)
    offset = dot(before.astype(jnp.float32), number).astype(jnp.int32)
    lane = lax.broadcasted_iota(jnp.int32, (steps, LAT), 1)
    step_of = lax.broadcasted_iota(jnp.int32, (steps, LAT), 0)
    reached = jnp.where((offset <= lane * LAT + (LAT - 1)) & (step_of <= LON), 1, 0)
    last_rows[...] = jnp.broadcast_to(jnp.sum(reached, axis=0, keepdims=True) - 1, (8, LAT))
    copy_last = pltpu.make_async_copy(last_rows, last, last_sem)
    copy_last.start()
    first_ref[...] = jnp.minimum(offset // LAT, TILES - 1)
    shift = offset % LAT
    for t in range(steps // 8):
        some = slice(8 * t, 8 * t + 8)
        ranks, moved_by = rank[some], shift[some]
        lanes = lane[some]
        wanted = ((lanes - moved_by + LAT) % LAT).astype(jnp.float32)
        position = jnp.zeros((8, LAT), jnp.int32)
        for half in (64, 32, 16, 8, 4, 2, 1):
            probe = jnp.take_along_axis(ranks, position + (half - 1), axis=1)
            position = jnp.where(probe <= wanted, position + half, position)
        low = (lanes >= moved_by).astype(jnp.int32)
        over = (moved_by.astype(jnp.float32) + number[some] >= LAT).astype(jnp.int32)
        place = (moved_by + ranks.astype(jnp.int32) + (LAT - 1)) % LAT
        for u in range(8):
            i = 8 * t + u
            if i < LON:
                for ref, value in ((source, position), (low_ref, low), (cross, over), (place_ref, place)):
                    ref[i] = jnp.broadcast_to(value[u:u + 1, :], (8, LAT))
                r = (i - 1) % LON
                gust[i] = jnp.broadcast_to(wind_ref[r:r + 1, :], (8, LAT))

    lanes = lane[:8]
    first_cells, edge_cells = offset[1:2, :], offset[2:3, :]
    head[0] = (lanes < first_cells).astype(jnp.int32)
    head[1] = (lanes < edge_cells).astype(jnp.int32)
    head[2] = (lanes + LAT < edge_cells).astype(jnp.int32)

    def own(at):
        part = [bins_ref[:, at + LOCAL * p:at + LOCAL * (p + 1)] for p in range(GROUPS)]
        return jnp.where(me < 2, jnp.where(me == 0, part[0], part[1]), jnp.where(me == 2, part[2], part[3]))

    def columns_of(row):
        row = jnp.concatenate([row, jnp.zeros((1, 3 * LAT - LOCAL), jnp.float32)], axis=1)
        return [jnp.broadcast_to(row[:, LAT * b:LAT * (b + 1)], (LAT, LAT)).T for b in range(3)]

    at_lat, at_weight, at_growth = columns_of(bins_ref[:, :LOCAL]), columns_of(own(LOCAL)), columns_of(own(5 * LOCAL))
    for b in range(3):
        rows = min(LAT, PADDED - LAT * b)
        real = min(LAT, LOCAL - LAT * b)
        to = pl.ds(LAT * b, rows)
        along = cour_ref[pl.ds(LAT * b, real), :]
        if real < rows:
            along = jnp.concatenate([along, jnp.zeros((rows - real, LAT), jnp.float32)], axis=0)
        up, down_by = jnp.maximum(along, 0.0), jnp.minimum(along, 0.0)
        lat = at_lat[b][:rows]
        north, south = jnp.maximum(lat, 0.0), jnp.minimum(lat, 0.0)
        lanes = lax.broadcasted_iota(jnp.int32, (rows, LAT), 1)
        coef[0, to, :] = 1.0 - up + down_by - north + south
        coef[1, to, :] = up
        coef[2, to, :] = -down_by
        coef[3, to, :] = jnp.where(lanes == 0, 0.0, north)
        coef[4, to, :] = jnp.where(lanes == LAT - 1, 0.0, -south)
        coef[5, to, :] = at_weight[b][:rows]
        grow[to, :] = at_growth[b][:rows]

    steep[...] = jnp.zeros_like(steep)
    pad = PADDED - LOCAL
    x[:, pl.ds(LOCAL, pad), :] = jnp.zeros((LON + 2, pad, LAT), jnp.float32)
    for p in range(GROUPS):
        tail[p, :, pl.ds(SIZES[-1] - pad, pad), :] = jnp.zeros((OWN, pad, LAT), jnp.float32)
    packed[pl.ds(0, 2)] = jnp.zeros((2,) + packed.shape[1:], jnp.float32)

    def tiles_of(start, n, base):
        at = [pl.ds(pl.multiple_of(base + 8 * j, 8), 8) for j in range(n)]
        to = [pl.ds(pl.multiple_of(base - start + 8 * j, 8), 8) for j in range(n)]
        return at, to, [[coef[q, at[j], :] for q in range(6)] for j in range(n)]

    def masked(row, rows):
        return x[row, rows, :] * sea[row]

    def upwind(coefs, low_side, mid, high_side, land):
        c0, cw, ce, cs, cn, _ = coefs
        value = c0 * mid + cw * low_side + ce * high_side
        value = value + cs * pltpu.roll(mid, 1, 1) + cn * pltpu.roll(mid, LAT - 1, 1)
        return value * land

    def inner(start, n, base):
        at, to, coefs = tiles_of(start, n, base)

        def treat(steps, sides, hold):
            stores = []
            for i in steps:
                land, turn, low, over, total = sea[i], source[i], low_ref[i] != 0, cross[i] != 0, steep[i]
                new_hold = []
                for j in range(n):
                    low_side, mid = sides[j]
                    high_side = masked(i + 1, at[j])
                    value = upwind(coefs[j], low_side, mid, high_side, land)
                    total = total + coefs[j][5] * value
                    turned = jnp.take_along_axis(value, turn, axis=1)
                    kept = jnp.where(low, turned, hold[j])
                    stores.append((moved, i - 1, at[j], value))
                    stores.append((packed, i, to[j], kept))
                    new_hold.append(jnp.where(over, turned, kept))
                    sides[j] = (mid, high_side)
                stores.append((steep, i, slice(None), total))
                hold = new_hold
            for ref, i, rows, value in stores:
                ref[i, rows, :] = value
            return sides, hold

        def several(s, carry):
            sides, hold = treat(
                [2 + s * ROWS_AT_ONCE + u for u in range(ROWS_AT_ONCE)], list(carry[0]), list(carry[1])
            )
            return (tuple(sides), tuple(hold))

        sides = tuple((masked(1, at[j]), masked(2, at[j])) for j in range(n))
        hold = tuple(jnp.zeros((8, LAT), jnp.float32) for j in range(n))
        count = (LON - 2) // ROWS_AT_ONCE
        sides, hold = lax.fori_loop(0, count, several, (sides, hold))
        _, hold = treat(list(range(2 + count * ROWS_AT_ONCE, LON)), list(sides), list(hold))
        for j in range(n):
            packed[LON, to[j], :] = hold[j]

    def outer(start, n, base):
        at, to, coefs = tiles_of(start, n, base)
        first_cells = head[0] != 0
        totals = [steep[0], steep[1]]
        stores = []
        for j in range(n):
            turned = []
            for i, row in ((0, LON), (1, 1)):
                value = upwind(coefs[j], masked(row - 1, at[j]), masked(row, at[j]), masked(row + 1, at[j]), sea[row])
                totals[i] = totals[i] + coefs[j][5] * value
                stores.append((moved, row - 1, at[j], value))
                turned.append(jnp.take_along_axis(value, source[i], axis=1))
            stores.append((edge, 0, to[j], jnp.where(first_cells, turned[0], turned[1])))
            stores.append((edge, 1, to[j], turned[1]))
        for ref, i, rows, value in stores:
            ref[i, rows, :] = value
        steep[0], steep[1] = totals

    def landing(c):
        if c == PARTS - 1:
            return tail.at[me]
        return recv.at[:, pl.ds(pl.multiple_of(KSTARTS[c] + me * SIZES[c], 8), SIZES[c]), :]

    sends = {}

    def send(c, half):
        start, size = STARTS[c], SIZES[c]
        rows = min(size, LOCAL - start)
        tiles = pl.ds(HALF * (1 - half), HALF)
        for d in (2, 1, 3):
            copy = pltpu.make_async_remote_copy(
                src_ref=stage.at[d - 1, tiles, pl.ds(start, rows), :],
                dst_ref=landing(c).at[tiles, pl.ds(0, rows), :],
                send_sem=send_sem.at[half, c, d - 1], recv_sem=recv_sem.at[half, c, d - 1],
                device_id=(block, peer(d)), device_id_type=MESH,
            )
            copy.start()
            sends[half, c, d] = copy

    edges = []
    for c in range(PARTS):
        start, size = STARTS[c], SIZES[c]
        n = 2 if size % 16 == 0 else 3
        loads[c].wait()

        def group(s, _, start=start, n=n):
            inner(start, n, start + s * 8 * n)
            return 0

        lax.fori_loop(0, size // (8 * n), group, 0)
        if c == 0:
            copy_last.wait()
        mine = landing(c)
        for d in (2, 1, 3, 0):
            to = peer(d)
            values = [
                packed[last[0, to * OWN + k], pl.ds(0, size), :] for k in range(OWN)
            ]
            for k in range(OWN):
                if d == 0:
                    mine[k] = values[k]
                else:
                    stage[d - 1, k, pl.ds(start, size), :] = values[k]
        if c == 0:
            pl.semaphore_wait(barrier, 5)
            for slot, row, into, to in ((0, LON - 1, 0, east), (1, 0, LON + 1, west)):
                for k, src, dst in (
                    (slot, spec_ref.at[row], x.at[into, pl.ds(0, LOCAL), :]),
                    (2 + slot, sea.at[row + 1], sea.at[into]),
                ):
                    copy = pltpu.make_async_remote_copy(
                        src_ref=src, dst_ref=dst, send_sem=halo_send.at[k], recv_sem=halo_recv.at[k],
                        device_id=(to, me), device_id_type=MESH,
                    )
                    copy.start()
                    edges.append(copy)
        send(c, 0)

    for copy in edges:
        copy.wait()
    for c in range(PARTS):
        start, size = STARTS[c], SIZES[c]
        n = 2 if size % 16 == 0 else 3

        def group(s, _, start=start, n=n):
            outer(start, n, start + s * 8 * n)
            return 0

        lax.fori_loop(0, size // (8 * n), group, 0)
        for d in (2, 1, 3, 0):
            here = jnp.where(peer(d) == 0, 1, 0)
            share = landing(c) if d == 0 else stage.at[d - 1, :, pl.ds(start, size), :]
            for k in range(2):
                old = share[k]
                use = jnp.broadcast_to((head[1 + k] * here)[:1, :], (size, LAT)) != 0
                new = jnp.where(use, edge[k, pl.ds(0, size), :], old)
                share[k] = new
        send(c, 1)

    sums[0] = jnp.sum(steep[...], axis=1)
    sum_copies = []
    for d in (1, 2, 3):
        copy = pltpu.make_async_remote_copy(
            src_ref=sums.at[0], dst_ref=sums.at[d], send_sem=sum_send.at[d - 1], recv_sem=sum_recv.at[d - 1],
            device_id=(block, peer(d)), device_id_type=MESH,
        )
        copy.start()
        sum_copies.append(copy)

    exact = functools.partial(jnp.dot, precision=lax.Precision.HIGHEST, preferred_element_type=jnp.float32)
    fcols[...] = exact(fmix_ref[...], fcol_ref[...])
    spread = time_step * exact(dmix_ref[...], dcol_ref[...])
    for j in range(4):
        dcols[pl.ds(j * ND, ND), :] = spread

    def matrix_rows(p, _):
        for g, (size, count) in enumerate(((144, 4), (144, 4), (48, 1))):
            for c in range(PARTS):
                width = GROUPS * SIZES[c]
                cols = pl.ds(KSTARTS[c], width)
                index = lax.broadcasted_iota(jnp.int32, (size, width), 0)
                rows = [fcols[pl.ds(p * 9 + 4 * g + j, 1), cols] for j in range(count)]
                if count == 1:
                    factor = jnp.where(index < ND, rows[0], 0.0)
                else:
                    factor = jnp.where(
                        index < 2 * ND,
                        jnp.where(index < ND, rows[0], rows[1]),
                        jnp.where(index < 3 * ND, rows[2], rows[3]),
                    )
                value = factor * dcols[pl.ds(0, size), cols]
                high = value.astype(jnp.bfloat16)
                low = (value - high.astype(jnp.float32)).astype(jnp.bfloat16)
                at = pl.ds(144 * g, size)
                w_hi[p, at, cols] = high
                w_lo[p, at, cols] = low
        return 0

    lax.fori_loop(0, GROUPS, matrix_rows, 0)

    def arrive(half):
        for c in range(PARTS):
            for d in (1, 2, 3):
                sends[half, c, d].wait_recv()

    def mix(half):
        for s in range(HALF // 2):
            k = HALF * (1 - half) + 2 * s
            for c in range(PARTS):
                rows = pl.ds(KSTARTS[c], GROUPS * SIZES[c])
                if c == PARTS - 1:
                    both = [jnp.concatenate([tail[p, k + u] for p in range(GROUPS)], axis=0) for u in range(2)]
                else:
                    both = [recv[k + u, rows, :] for u in range(2)]
                value = jnp.concatenate(both, axis=1)
                high = value.astype(jnp.bfloat16)
                f_hi[rows, :] = high
                f_lo[rows, :] = (value - high.astype(jnp.float32)).astype(jnp.bfloat16)

            def rows_of(p, _, k=k):
                value = dot(w_hi[p], f_hi[...]) + dot(w_lo[p], f_hi[...]) + dot(w_hi[p], f_lo[...])
                acc[p, k] = value[:, :LAT]
                acc[p, k + 1] = value[:, LAT:]
                return 0

            lax.fori_loop(0, GROUPS, rows_of, 0)

    backs = []

    def send_back(half, d):
        p = peer(d)
        src = acc.at[p, pl.ds(HALF * (1 - half), HALF), pl.ds(0, LOCAL), :]
        tiles = pl.ds(me * OWN + HALF * (1 - half), HALF)
        if d == 0:
            copy = pltpu.make_async_copy(src, mixed_ref.at[tiles], own_sem.at[half])
        else:
            copy = pltpu.make_async_remote_copy(
                src_ref=src, dst_ref=mixed_ref.at[tiles],
                send_sem=back_send.at[half, d - 1], recv_sem=back_recv.at[half, d - 1],
                device_id=(block, p), device_id_type=MESH,
            )
        copy.start()
        backs.append(copy)

    arrive(0)
    mix(0)
    send_back(0, 2)
    arrive(1)
    for d in (1, 3, 0):
        send_back(0, d)
    mix(1)
    for d in (2, 1, 3, 0):
        send_back(1, d)

    for copy in sum_copies:
        copy.wait()
    whole = (sums[0] + sums[1]) + (sums[2] + sums[3])
    whole = dissipation * whole / (1.0 + whole)
    for i in range(LON):
        damp[i] = jnp.broadcast_to(whole[i:i + 1, :], (8, LAT))

    def add_own(i, row):
        keep = time_step * live_ref[i]
        gusts, damps = gust[i], damp[i]
        values = []
        for t in range(PADDED // 8):
            value = moved[row, pl.ds(8 * t, 8), :]
            values.append(value + keep * (value * (grow[pl.ds(8 * t, 8), :] * gusts - damps)))
        for t in range(PADDED // 8):
            moved[row, pl.ds(8 * t, 8), :] = values[t]

    def rows_own(i, _):
        add_own(i, i - 1)
        return 0

    lax.fori_loop(1, LON, rows_own, 0)
    add_own(0, LON - 1)
    store = pltpu.make_async_copy(moved.at[:, pl.ds(0, LOCAL), :], moved_ref, out_sem)
    store.start()
    store.wait()
    for copy in sends.values():
        copy.wait_send()
    for copy in backs:
        copy.wait()


def finish_kernel(first_ref, moved_ref, mixed_ref, live_ref, low_ref, place_ref, out_ref):
    tiles = moved_ref.shape[1] // 8

    def treat(todo):
        stores = []
        for i, row in todo:
            first = first_ref[i, 0]
            after = jnp.minimum(first + 1, TILES - 1)
            low, place, live = low_ref[i] != 0, place_ref[i], live_ref[i] != 0.0
            for j in range(tiles):
                at = pl.ds(8 * j, 8)
                joined = jnp.where(low, mixed_ref[first, at, :], mixed_ref[after, at, :])
                term = jnp.take_along_axis(joined, place, axis=1)
                stores.append((row, at, moved_ref[row, at, :] + jnp.where(live, term, 0.0)))
        for row, at, value in stores:
            out_ref[row, at, :] = value

    def several(s, _):
        treat([(s * 4 + u + 1, s * 4 + u) for u in range(4)])
        return 0

    lax.fori_loop(0, (LON - 1) // 4, several, 0)
    treat([(0, LON - 1)])


def on_device(
    spectrum, sea_mask, cour_lon, cour_lat, wind, growth_rate, band_weight, freq_mix, dir_mix, routes, counts
):
    spec = jnp.transpose(spectrum, (1, 0, 2))
    fcol, dcol = column_maps()
    f32, bf16, i32 = jnp.float32, jnp.bfloat16, jnp.int32
    vmem = pl.BlockSpec(memory_space=pltpu.VMEM)
    hbm = pl.BlockSpec(memory_space=pl.ANY)
    smem = pl.BlockSpec(memory_space=pltpu.SMEM)
    dma = pltpu.SemaphoreType.DMA
    wide = (LON, 8, LAT)
    moved, mixed, live, low, place, first = pl.pallas_call(
        exchange_kernel,
        out_shape=(
            jax.ShapeDtypeStruct((LON, LOCAL, LAT), f32),
            jax.ShapeDtypeStruct((TILES, LOCAL, LAT), f32),
            jax.ShapeDtypeStruct(wide, f32),
            jax.ShapeDtypeStruct(wide, i32),
            jax.ShapeDtypeStruct(wide, i32),
            jax.ShapeDtypeStruct((LON + 3, LAT), i32),
        ),
        in_specs=[hbm] + [vmem] * 8,
        out_specs=(hbm, hbm) + (vmem,) * 4,
        scratch_shapes=[
            pltpu.VMEM((LON + 2, PADDED, LAT), f32),
            pltpu.VMEM((LON, PADDED, LAT), f32),
            pltpu.VMEM((LON + 2, 8, LAT), f32),
            pltpu.VMEM(wide, f32),
            pltpu.VMEM(wide, f32),
            pltpu.VMEM(wide, i32),
            pltpu.VMEM(wide, i32),
            pltpu.VMEM((3, 8, LAT), i32),
            pltpu.VMEM((LON + 3, LAT), f32),
            pltpu.VMEM((8, LAT), i32),
            pltpu.SMEM((8, LAT), i32),
            pltpu.VMEM((6, PADDED, LAT), f32),
            pltpu.VMEM((PADDED, LAT), f32),
            pltpu.VMEM((LON + 1, max(SIZES), LAT), f32),
            pltpu.VMEM((2, max(SIZES), LAT), f32),
            pltpu.VMEM((GROUPS - 1, OWN, PADDED, LAT), f32),
            pltpu.VMEM((OWN, KSTARTS[-1], LAT), f32),
            pltpu.VMEM((GROUPS, OWN, SIZES[-1], LAT), f32),
            pltpu.VMEM((GROUPS, OWN, MROWS, LAT), f32),
            pltpu.VMEM((GROUPS, MROWS, KTOTAL), bf16),
            pltpu.VMEM((GROUPS, MROWS, KTOTAL), bf16),
            pltpu.VMEM((KTOTAL, 256), bf16),
            pltpu.VMEM((KTOTAL, 256), bf16),
            pltpu.VMEM((NF, KTOTAL), f32),
            pltpu.VMEM((4 * ND, KTOTAL), f32),
            pltpu.VMEM(wide, f32),
            pltpu.VMEM((GROUPS, LON, LAT), f32),
            dma((PARTS,)), dma((4,)), dma((4,)), dma((2, PARTS, 3)), dma((2, PARTS, 3)),
            dma((2, 3)), dma((2, 3)), dma((3,)), dma((3,)), dma((2,)), dma, dma,
        ],
        compiler_params=pltpu.CompilerParams(
            collective_id=0, has_side_effects=True, vmem_limit_bytes=56 << 20
        ),
    )(
        spec, sea_mask, cour_lon, wind,
        jnp.concatenate([cour_lat, band_weight, growth_rate]).reshape(1, -1), freq_mix, dir_mix, jnp.asarray(fcol), jnp.asarray(dcol),
    )
    step = 88
    whole = pl.BlockSpec(wide, lambda c: (0, 0, 0))
    out = pl.pallas_call(
        finish_kernel,
        out_shape=jax.ShapeDtypeStruct((LON, LOCAL, LAT), f32),
        grid=(pl.cdiv(LOCAL, step),),
        in_specs=[
            smem,
            pl.BlockSpec((LON, step, LAT), lambda c: (0, c, 0)),
            pl.BlockSpec((TILES, step, LAT), lambda c: (0, c, 0)),
            whole, whole, whole,
        ],
        out_specs=pl.BlockSpec((LON, step, LAT), lambda c: (0, c, 0)),
        compiler_params=pltpu.CompilerParams(vmem_limit_bytes=58 << 20),
    )(first, moved, mixed, live, low, place)
    return jnp.transpose(out, (1, 0, 2))


def solution(mesh):
    placed = (
        P("bin", "lon", None),
        P("lon", None),
        P("bin", None),
        P("bin"),
        P("lon", None),
        P(),
        P(),
        P(),
        P(),
        P("lon", None, None),
        P("lon", None),
    )
    return jax.shard_map(
        on_device, mesh=mesh, in_specs=placed, out_specs=P("bin", "lon", None), check_vma=False
    )
```

time: 149 us -> 140 us (0.940)
  Pallas kernels: 145 us -> 138 us
  local copies, waits for them, and re-layouts: 3.84 us -> 1.42 us
    pallas_call x1, Pallas kernels: 133 us -> 127 us  [on_device(): pl.pallas_call(exchange_kernel, out_shape=(jax.ShapeDtypeStruct((LON, LOC...]
    reshape x3 -> x1, local copies, waits for them, and re-layouts: 3.84 us -> 0.61 us  [on_device(): jnp.concatenate([cour_lat, band_weight, growth_rate]).reshape(1, -1)]
where the time goes in v3:
time: 140 us
  Pallas kernels  138 us (99%)
  local copies, waits for them, and re-layouts  1.42 us (1%)
    pallas_call x1, Pallas kernels, on_device(): pl.pallas_call(exchange_kernel, out_shape=(jax.ShapeDtypeStruct((LON, LOC...  127 us
    pallas_call x1, Pallas kernels, on_device(): pl.pallas_call(finish_kernel, out_shape=jax.ShapeDtypeStruct((LON, LOCAL,...  11.1 us

profile of v3, /device:TPU:1, one launch (start us, length us, event | category | flops | bytes accessed | tf_op | source)
XLA Modules:
  0.0 139.9 jit_solution(16273877224288655608)
XLA Ops:
  0.0 0.8 concatenate.3
  0.8 0.6 reshape.3.bins_ref
  1.4 127.4 %shard_map.109 = (f32[45,324,128]{2,1,0:T(8,128)}, f32[32,324,128]{2,1,0:T(8,128)}, f32[45,8,128]{2,1,0:T(8,128)}, s32[45,8,128]{2,1,0:T(8,128)}, s32[45,8,128]{2,1,0:T(8,128)}, /*index=5*/s32[48,128]{1,0:T(8,128)}) custom-call(f32[45,324,128]{2,1,0:T(8,128)} %bitcast.2, s32[45,128]{1,0:T(8,128)} %mask_ref.1, f32[324,128]{1,0:T(8,128)} %cour_ref.1, ...), custom_call_target="tpu_custom_call" | custom-call | tf_op jit(solution)/shard_map/pallas_call | solution.py:483
  128.8 11.1 %shard_map.110 = f32[45,324,128]{2,1,0:T(8,128)} custom-call(s32[48,128]{1,0:T(8,128)} %get-tuple-element.11.first_ref, f32[45,324,128]{2,1,0:T(8,128)} %get-tuple-element.12.moved_ref, f32[32,324,128]{2,1,0:T(8,128)} %get-tuple-element.13.mixed_ref, f32[45,8,128]{2,1,0:T(8,128)} %get-tuple-element.14.live_ref, s32[45,8,128]{2,1,0:T(8,128)} %get-tuple-element.15.low_ref, ...), custom_call_target="tpu_custom_call" | custom-call | tf_op jit(solution)/shard_map/pallas_call | solution.py:535

commit v4 on v3

--- a/solution.py
+++ b/solution.py
@@ -19,8 +19,8 @@
 CELLS = 4096
 SHARE = CELLS // GROUPS
 TILES = CELLS // LAT
-SIZES = (64, 64, 64, 64, 72)
-STARTS = (0, 64, 128, 192, 256)
+SIZES = (16, 32, 48, 96, 136)
+STARTS = (0, 16, 48, 96, 192)
 PARTS = len(SIZES)
 KSTARTS = tuple(GROUPS * s for s in STARTS)
 KTOTAL = GROUPS * PADDED
@@ -46,11 +46,13 @@
 
 
 def exchange_kernel(
-    spec_ref, mask_ref, cour_ref, wind_ref, bins_ref, fmix_ref, dmix_ref, fcol_ref, dcol_ref,
-    moved_ref, mixed_ref, live_ref, low_ref, place_ref, first_ref,
+    spec_ref, mask_ref, cour_hbm, wind_ref, bins_ref, fmix_ref, dmix_ref, fcol_hbm, dcol_hbm,
+    moved_ref, mixed_ref, live_out, low_out, place_out, first_out,
+    cour_ref, fcol_ref, dcol_ref, live_ref, low_ref, place_ref, first_ref,
     x, moved, sea, gust, damp, source, cross, head, order, last_rows, last, coef, grow, packed, edge, stage, recv, tail, acc,
     w_hi, w_lo, f_hi, f_lo, fcols, dcols, steep, sums,
     in_sem, halo_send, halo_recv, send_sem, recv_sem, back_send, back_recv, sum_send, sum_recv, own_sem, last_sem, out_sem,
+    early_sem, late_sem,
 ):
     me = lax.axis_index("bin")
     block = lax.axis_index("lon")
@@ -66,6 +68,12 @@
         pl.semaphore_signal(barrier, inc=1, device_id=(block, peer(d)), device_id_type=MESH)
     pl.semaphore_signal(barrier, inc=1, device_id=(west, me), device_id_type=MESH)
     pl.semaphore_signal(barrier, inc=1, device_id=(east, me), device_id_type=MESH)
+
+    early = [
+        pltpu.make_async_copy(src, dst, early_sem.at[q])
+        for q, (src, dst) in enumerate(((cour_hbm, cour_ref), (fcol_hbm, fcol_ref), (dcol_hbm, dcol_ref)))
+    ]
+    early[0].start()
 
     loads = []
     for c in range(PARTS):
@@ -77,6 +85,9 @@
         )
         copy.start()
         loads.append(copy)
+
+    for copy in early[1:]:
+        copy.start()
 
     flags = mask_ref[...].astype(jnp.float32)
     for r in range(LON):
@@ -124,6 +135,15 @@
                 r = (i - 1) % LON
                 gust[i] = jnp.broadcast_to(wind_ref[r:r + 1, :], (8, LAT))
 
+    late = [
+        pltpu.make_async_copy(src, dst, late_sem.at[q])
+        for q, (src, dst) in enumerate(
+            ((live_ref, live_out), (low_ref, low_out), (place_ref, place_out), (first_ref, first_out))
+        )
+    ]
+    for copy in late:
+        copy.start()
+
     lanes = lane[:8]
     first_cells, edge_cells = offset[1:2, :], offset[2:3, :]
     head[0] = (lanes < first_cells).astype(jnp.int32)
@@ -138,6 +158,7 @@
         row = jnp.concatenate([row, jnp.zeros((1, 3 * LAT - LOCAL), jnp.float32)], axis=1)
         return [jnp.broadcast_to(row[:, LAT * b:LAT * (b + 1)], (LAT, LAT)).T for b in range(3)]
 
+    early[0].wait()
     at_lat, at_weight, at_growth = columns_of(bins_ref[:, :LOCAL]), columns_of(own(LOCAL)), columns_of(own(5 * LOCAL))
     for b in range(3):
         rows = min(LAT, PADDED - LAT * b)
@@ -165,9 +186,12 @@
         tail[p, :, pl.ds(SIZES[-1] - pad, pad), :] = jnp.zeros((OWN, pad, LAT), jnp.float32)
     packed[pl.ds(0, 2)] = jnp.zeros((2,) + packed.shape[1:], jnp.float32)
 
+    def tile_rows(first):
+        return pl.ds(first if isinstance(first, int) else pl.multiple_of(first, 8), 8)
+
     def tiles_of(start, n, base):
-        at = [pl.ds(pl.multiple_of(base + 8 * j, 8), 8) for j in range(n)]
-        to = [pl.ds(pl.multiple_of(base - start + 8 * j, 8), 8) for j in range(n)]
+        at = [tile_rows(base + 8 * j) for j in range(n)]
+        to = [tile_rows(base - start + 8 * j) for j in range(n)]
         return at, to, [[coef[q, at[j], :] for q in range(6)] for j in range(n)]
 
     def masked(row, rows):
@@ -241,6 +265,17 @@
             return tail.at[me]
         return recv.at[:, pl.ds(pl.multiple_of(KSTARTS[c] + me * SIZES[c], 8), SIZES[c]), :]
 
+    def for_all_tiles(treat, start, size):
+        odd = 3 * (size // 8 % 2)
+
+        def pair(s, _):
+            treat(start, 2, start + s * 16)
+            return 0
+
+        lax.fori_loop(0, (size // 8 - odd) // 2, pair, 0)
+        if odd:
+            treat(start, odd, start + size - 8 * odd)
+
     sends = {}
 
     def send(c, half):
@@ -260,14 +295,8 @@
     edges = []
     for c in range(PARTS):
         start, size = STARTS[c], SIZES[c]
-        n = 2 if size % 16 == 0 else 3
         loads[c].wait()
-
-        def group(s, _, start=start, n=n):
-            inner(start, n, start + s * 8 * n)
-            return 0
-
-        lax.fori_loop(0, size // (8 * n), group, 0)
+        for_all_tiles(inner, start, size)
         if c == 0:
             copy_last.wait()
         mine = landing(c)
@@ -300,13 +329,7 @@
         copy.wait()
     for c in range(PARTS):
         start, size = STARTS[c], SIZES[c]
-        n = 2 if size % 16 == 0 else 3
-
-        def group(s, _, start=start, n=n):
-            outer(start, n, start + s * 8 * n)
-            return 0
-
-        lax.fori_loop(0, size // (8 * n), group, 0)
+        for_all_tiles(outer, start, size)
         for d in (2, 1, 3, 0):
             here = jnp.where(peer(d) == 0, 1, 0)
             share = landing(c) if d == 0 else stage.at[d - 1, :, pl.ds(start, size), :]
@@ -328,6 +351,8 @@
         sum_copies.append(copy)
 
     exact = functools.partial(jnp.dot, precision=lax.Precision.HIGHEST, preferred_element_type=jnp.float32)
+    for copy in early[1:]:
+        copy.wait()
     fcols[...] = exact(fmix_ref[...], fcol_ref[...])
     spread = time_step * exact(dmix_ref[...], dcol_ref[...])
     for j in range(4):
@@ -335,9 +360,9 @@
 
     def matrix_rows(p, _):
         for g, (size, count) in enumerate(((144, 4), (144, 4), (48, 1))):
-            for c in range(PARTS):
-                width = GROUPS * SIZES[c]
-                cols = pl.ds(KSTARTS[c], width)
+            for first in range(0, KTOTAL - 255, 256):
+                width = 256 if first + 512 <= KTOTAL else KTOTAL - first
+                cols = pl.ds(first, width)
                 index = lax.broadcasted_iota(jnp.int32, (size, width), 0)
                 rows = [fcols[pl.ds(p * 9 + 4 * g + j, 1), cols] for j in range(count)]
                 if count == 1:
@@ -437,6 +462,8 @@
     add_own(0, LON - 1)
     store = pltpu.make_async_copy(moved.at[:, pl.ds(0, LOCAL), :], moved_ref, out_sem)
     store.start()
+    for copy in late:
+        copy.wait()
     store.wait()
     for copy in sends.values():
         copy.wait_send()
@@ -490,9 +517,16 @@
             jax.ShapeDtypeStruct(wide, i32),
             jax.ShapeDtypeStruct((LON + 3, LAT), i32),
         ),
-        in_specs=[hbm] + [vmem] * 8,
-        out_specs=(hbm, hbm) + (vmem,) * 4,
+        in_specs=[hbm, vmem, hbm] + [vmem] * 4 + [hbm, hbm],
+        out_specs=(hbm,) * 6,
         scratch_shapes=[
+            pltpu.VMEM((LOCAL, LAT), f32),
+            pltpu.VMEM((NF, KTOTAL), f32),
+            pltpu.VMEM((ND, KTOTAL), f32),
+            pltpu.VMEM(wide, f32),
+            pltpu.VMEM(wide, i32),
+            pltpu.VMEM(wide, i32),
+            pltpu.VMEM((LON + 3, LAT), i32),
             pltpu.VMEM((LON + 2, PADDED, LAT), f32),
             pltpu.VMEM((LON, PADDED, LAT), f32),
             pltpu.VMEM((LON + 2, 8, LAT), f32),
@@ -522,6 +556,7 @@
             pltpu.VMEM((GROUPS, LON, LAT), f32),
             dma((PARTS,)), dma((4,)), dma((4,)), dma((2, PARTS, 3)), dma((2, PARTS, 3)),
             dma((2, 3)), dma((2, 3)), dma((3,)), dma((3,)), dma((2,)), dma, dma,
+            dma((3,)), dma((4,)),
         ],
         compiler_params=pltpu.CompilerParams(
             collective_id=0, has_side_effects=True, vmem_limit_bytes=56 << 20

time: 140 us -> 138 us (0.986)
  Pallas kernels: 138 us -> 136 us
    pallas_call x1, Pallas kernels: 127 us -> 125 us  [on_device(): pl.pallas_call(exchange_kernel, out_shape=(jax.ShapeDtypeStruct((LON, LOC...]
where the time goes in v4:
time: 138 us
  Pallas kernels  136 us (99%)
  local copies, waits for them, and re-layouts  1.42 us (1%)
    pallas_call x1, Pallas kernels, on_device(): pl.pallas_call(exchange_kernel, out_shape=(jax.ShapeDtypeStruct((LON, LOC...  125 us
    pallas_call x1, Pallas kernels, on_device(): pl.pallas_call(finish_kernel, out_shape=jax.ShapeDtypeStruct((LON, LOCAL,...  11.1 us

profile of v4, /device:TPU:1, one launch (start us, length us, event | category | flops | bytes accessed | tf_op | source)
XLA Modules:
  0.0 137.8 jit_solution(12653448405714245072)
XLA Ops:
  0.0 0.8 concatenate.3
  0.8 0.6 reshape.3.bins_ref
  1.4 125.2 %shard_map.109 = (f32[45,324,128]{2,1,0:T(8,128)}, f32[32,324,128]{2,1,0:T(8,128)}, f32[45,8,128]{2,1,0:T(8,128)}, s32[45,8,128]{2,1,0:T(8,128)}, s32[45,8,128]{2,1,0:T(8,128)}, /*index=5*/s32[48,128]{1,0:T(8,128)}) custom-call(f32[45,324,128]{2,1,0:T(8,128)} %bitcast.2, s32[45,128]{1,0:T(8,128)} %mask_ref.1, f32[324,128]{1,0:T(8,128)} %cour_hbm.1, ...), custom_call_target="tpu_custom_call" | custom-call | tf_op jit(solution)/shard_map/pallas_call | solution.py:510
  126.7 11.1 %shard_map.110 = f32[45,324,128]{2,1,0:T(8,128)} custom-call(s32[48,128]{1,0:T(8,128)} %get-tuple-element.11.first_ref, f32[45,324,128]{2,1,0:T(8,128)} %get-tuple-element.12.moved_ref, f32[32,324,128]{2,1,0:T(8,128)} %get-tuple-element.13.mixed_ref, f32[45,8,128]{2,1,0:T(8,128)} %get-tuple-element.14.live_ref, s32[45,8,128]{2,1,0:T(8,128)} %get-tuple-element.15.low_ref, ...), custom_call_target="tpu_custom_call" | custom-call | tf_op jit(solution)/shard_map/pallas_call | solution.py:570

commit v5 on v4

--- a/solution.py
+++ b/solution.py
@@ -46,7 +46,7 @@
 
 
 def exchange_kernel(
-    spec_ref, mask_ref, cour_hbm, wind_ref, bins_ref, fmix_ref, dmix_ref, fcol_hbm, dcol_hbm,
+    spec_ref, mask_ref, cour_hbm, wind_ref, lat_ref, weight_ref, growth_ref, fmix_ref, dmix_ref, fcol_hbm, dcol_hbm,
     moved_ref, mixed_ref, live_out, low_out, place_out, first_out,
     cour_ref, fcol_ref, dcol_ref, live_ref, low_ref, place_ref, first_ref,
     x, moved, sea, gust, damp, source, cross, head, order, last_rows, last, coef, grow, packed, edge, stage, recv, tail, acc,
@@ -150,8 +150,9 @@
     head[1] = (lanes < edge_cells).astype(jnp.int32)
     head[2] = (lanes + LAT < edge_cells).astype(jnp.int32)
 
-    def own(at):
-        part = [bins_ref[:, at + LOCAL * p:at + LOCAL * (p + 1)] for p in range(GROUPS)]
+    def own(ref):
+        row = ref[...].reshape(1, GROUPS * LOCAL)
+        part = [row[:, LOCAL * p:LOCAL * (p + 1)] for p in range(GROUPS)]
         return jnp.where(me < 2, jnp.where(me == 0, part[0], part[1]), jnp.where(me == 2, part[2], part[3]))
 
     def columns_of(row):
@@ -159,7 +160,7 @@
         return [jnp.broadcast_to(row[:, LAT * b:LAT * (b + 1)], (LAT, LAT)).T for b in range(3)]
 
     early[0].wait()
-    at_lat, at_weight, at_growth = columns_of(bins_ref[:, :LOCAL]), columns_of(own(LOCAL)), columns_of(own(5 * LOCAL))
+    at_lat, at_weight, at_growth = columns_of(lat_ref[...].reshape(1, LOCAL)), columns_of(own(weight_ref)), columns_of(own(growth_ref))
     for b in range(3):
         rows = min(LAT, PADDED - LAT * b)
         real = min(LAT, LOCAL - LAT * b)
@@ -489,10 +490,10 @@
             out_ref[row, at, :] = value
 
     def several(s, _):
-        treat([(s * 4 + u + 1, s * 4 + u) for u in range(4)])
+        treat([(s * 11 + u + 1, s * 11 + u) for u in range(11)])
         return 0
 
-    lax.fori_loop(0, (LON - 1) // 4, several, 0)
+    lax.fori_loop(0, (LON - 1) // 11, several, 0)
     treat([(0, LON - 1)])
 
 
@@ -517,7 +518,7 @@
             jax.ShapeDtypeStruct(wide, i32),
             jax.ShapeDtypeStruct((LON + 3, LAT), i32),
         ),
-        in_specs=[hbm, vmem, hbm] + [vmem] * 4 + [hbm, hbm],
+        in_specs=[hbm, vmem, hbm] + [vmem] * 6 + [hbm, hbm],
         out_specs=(hbm,) * 6,
         scratch_shapes=[
             pltpu.VMEM((LOCAL, LAT), f32),
@@ -563,7 +564,7 @@
         ),
     )(
         spec, sea_mask, cour_lon, wind,
-        jnp.concatenate([cour_lat, band_weight, growth_rate]).reshape(1, -1), freq_mix, dir_mix, jnp.asarray(fcol), jnp.asarray(dcol),
+        cour_lat, band_weight, growth_rate, freq_mix, dir_mix, jnp.asarray(fcol), jnp.asarray(dcol),
     )
     step = 88
     whole = pl.BlockSpec(wide, lambda c: (0, 0, 0))

time: 138 us -> 135 us (0.978)
  local copies, waits for them, and re-layouts: 1.42 us -> 0 us
where the time goes in v5:
time: 135 us
  Pallas kernels  135 us (100%)
    pallas_call x1, Pallas kernels, on_device(): pl.pallas_call(exchange_kernel, out_shape=(jax.ShapeDtypeStruct((LON, LOC...  125 us
    pallas_call x1, Pallas kernels, on_device(): pl.pallas_call(finish_kernel, out_shape=jax.ShapeDtypeStruct((LON, LOCAL,...  9.92 us

profile of v5, /device:TPU:1, one launch (start us, length us, event | category | flops | bytes accessed | tf_op | source)
XLA Modules:
  0.0 135.1 jit_solution(8402366192290261332)
XLA Ops:
  0.0 125.2 %shard_map.109 = (f32[45,324,128]{2,1,0:T(8,128)}, f32[32,324,128]{2,1,0:T(8,128)}, f32[45,8,128]{2,1,0:T(8,128)}, s32[45,8,128]{2,1,0:T(8,128)}, s32[45,8,128]{2,1,0:T(8,128)}, /*index=5*/s32[48,128]{1,0:T(8,128)}) custom-call(f32[45,324,128]{2,1,0:T(8,128)} %bitcast.2, s32[45,128]{1,0:T(8,128)} %mask_ref.1, f32[324,128]{1,0:T(8,128)} %cour_hbm.1, ...), custom_call_target="tpu_custom_call" | custom-call | tf_op jit(solution)/shard_map/pallas_call | solution.py:511
  125.2 9.9 %shard_map.110 = f32[45,324,128]{2,1,0:T(8,128)} custom-call(s32[48,128]{1,0:T(8,128)} %get-tuple-element.11.first_ref, f32[45,324,128]{2,1,0:T(8,128)} %get-tuple-element.12.moved_ref, f32[32,324,128]{2,1,0:T(8,128)} %get-tuple-element.13.mixed_ref, f32[45,8,128]{2,1,0:T(8,128)} %get-tuple-element.14.live_ref, s32[45,8,128]{2,1,0:T(8,128)} %get-tuple-element.15.low_ref, ...), custom_call_target="tpu_custom_call" | custom-call | tf_op jit(solution)/shard_map/pallas_call | solution.py:571
